TPU v7x, 32 devices: a whole 2x2x4 slice. The times are simulated.
32 devices in a mesh: patch: 2 (over core), lat: 2 (over y), lon: 8 (over z, x).
Axes of the slice: x: 2, y: 2, z: 4, core: 2. Of those that a mesh axis runs over, the one named last changes fastest.
Arguments:
- velocity: float32 [2, 3, 32, 64, 128], P('patch', None, 'lat', 'lon'), may hold values from -6 to 6
- forcing: float32 [2, 3, 32, 64, 128], P('patch', None, 'lat', 'lon'), may hold values from -3 to 3
- viscosity: float32 [2, 32, 64, 128], P('patch', 'lat', 'lon'), may hold values from 1 to 10
- ghost_slots: int32 [2, 192], P('patch'), may hold values from 0 to 191, each once within a row
- corner_rows: int32 [2, 2, 96], P('patch', 'lat', 'lon'), may hold values from 0 to 15
- corner_cols: int32 [2, 2, 96], P('patch', 'lat', 'lon'), may hold values from 0 to 7
- corner_weights: float32 [2, 2, 4, 96], P('patch', 'lat', None, 'lon'), may hold values from 0 to 1, as said below
Outputs:
- new_velocity: float32 [2, 3, 32, 64, 128], P('patch', None, 'lat', 'lon')
- residual: float32 [2, 3, 32, 64, 128], P('patch', None, 'lat', 'lon')
Inputs may be any that keep to these rules, and one draw needn't show every extreme that they name: `ghost_slots`: each row names every slot of the other patch exactly once. `corner_rows`: the row below the corner is read too, from the next device or as zero beyond the patch. `corner_cols`: the column after the corner is read too, from the next device or as zero beyond the patch. `corner_weights`: the four weights of a slot are (1 - s)(1 - t), s(1 - t), (1 - s)t and st for some s and t in [0, 1).
All inputs are finite; a program needn't handle non-finite values.
Results may differ from a plain program's by a relative error of at most 0.0001.
Values sent between devices are 32-bit elements; how exact they have to be, the bound alone decides.
A program may use at most 64 MiB of HBM per device.

v0:
```python
import jax
import jax.numpy as jnp
from jax import lax
from jax.sharding import PartitionSpec as P

SWEEPS = 2
COARSE = 8


RELAX = 0.8


def with_halo(shard, sides, width):
    for axis, dim in sides:
        devices, length = (lax.axis_size(axis), shard.shape[dim])
        up = [(i, (i + 1) % devices) for i in range(devices - 1)]
        down = [(j, i) for i, j in up]
        last = lax.slice_in_dim(shard, length - width, length, axis=dim)
        first = lax.slice_in_dim(shard, 0, width, axis=dim)
        before = lax.ppermute(last, axis, up)
        after = lax.ppermute(first, axis, down)
        shard = jnp.concatenate([before, shard, after], axis=dim)
    return shard


def swapped(value, axis, apart):
    mask = 2**apart
    pairs = [(source, source ^ mask) for source in range(lax.axis_size(axis))]
    return lax.ppermute(value, axis, pairs)


def face_terms(padded_visc, weight_scale):
    centre = padded_visc[1:-1, 1:-1, 1:-1]
    return (
        weight_scale * (centre + padded_visc[:-2, 1:-1, 1:-1]),
        weight_scale * (centre + padded_visc[2:, 1:-1, 1:-1]),
        weight_scale * (centre + padded_visc[1:-1, :-2, 1:-1]),
        weight_scale * (centre + padded_visc[1:-1, 2:, 1:-1]),
        weight_scale * (centre + padded_visc[1:-1, 1:-1, :-2]),
        weight_scale * (centre + padded_visc[1:-1, 1:-1, 2:]),
    )


def diagonal_of(face_coefs):
    return (
        face_coefs[0]
        + face_coefs[1]
        + face_coefs[2]
        + face_coefs[3]
        + face_coefs[4]
        + face_coefs[5]
    )


def neighbour_sum(padded, face_coefs):
    summed = face_coefs[0] * padded[:, :-2, 1:-1, 1:-1]
    summed = summed + face_coefs[1] * padded[:, 2:, 1:-1, 1:-1]
    summed = summed + face_coefs[2] * padded[:, 1:-1, :-2, 1:-1]
    summed = summed + face_coefs[3] * padded[:, 1:-1, 2:, 1:-1]
    summed = summed + face_coefs[4] * padded[:, 1:-1, 1:-1, :-2]
    summed = summed + face_coefs[5] * padded[:, 1:-1, 1:-1, 2:]
    return summed


def bilinear(weight_rows, corner_list):
    summed = weight_rows[0][None, :, None] * corner_list[0]
    summed = summed + weight_rows[1][None, :, None] * corner_list[1]
    summed = summed + weight_rows[2][None, :, None] * corner_list[2]
    summed = summed + weight_rows[3][None, :, None] * corner_list[3]
    return summed


def clamp_take(source_array, along_dim, offset, block_size, whole_size, margin):
    position = offset + jnp.arange(-margin, block_size + margin, dtype=jnp.int32)
    picked = jnp.clip(position, 0, whole_size - 1) - offset + margin
    return jnp.take(source_array, picked, axis=along_dim)


def per_device(velocity, forcing, viscosity, ghost_slots, corner_rows, corner_cols, corner_weights):
    start_field = velocity[0]
    force_block = forcing[0]
    viscous = viscosity[0]
    row_block, col_block, levels = viscous.shape
    lat_count = lax.axis_size("lat")
    lon_count = lax.axis_size("lon")
    lat_index = lax.axis_index("lat")
    lon_index = lax.axis_index("lon")
    lat_cells = row_block * lat_count
    lon_cells = col_block * lon_count
    row_offset = lat_index * row_block
    col_offset = lon_index * col_block
    ghost_count = ghost_slots.shape[1]
    order_row = ghost_slots[0]
    rim_width = 1
    visc_rim = with_halo(viscous, (("lat", 0), ("lon", 1)), 2)
    visc_ext = clamp_take(visc_rim, 0, row_offset, row_block, lat_cells, 2)
    visc_ext = clamp_take(visc_ext, 1, col_offset, col_block, lon_cells, 2)
    visc_ext = jnp.pad(visc_ext, ((0, 0), (0, 0), (2, 2)), mode="edge")
    loop_coefs = face_terms(visc_ext[:, :, 1:-1], 0.5)
    loop_diag = diagonal_of(loop_coefs)
    loop_rows = row_offset + jnp.arange(-1, row_block + 1, dtype=jnp.int32)
    loop_cols = col_offset + jnp.arange(-1, col_block + 1, dtype=jnp.int32)
    loop_parity = (
        loop_rows[:, None, None]
        + loop_cols[None, :, None]
        + jnp.arange(levels, dtype=jnp.int32)[None, None, :]
    ) % 2
    loop_inside = (
        ((loop_rows >= 0) & (loop_rows < lat_cells))[:, None]
        & ((loop_cols >= 0) & (loop_cols < lon_cells))[None, :]
    )[:, :, None]
    ext_rows = row_offset + jnp.arange(-rim_width, row_block + rim_width, dtype=jnp.int32)
    ext_cols = col_offset + jnp.arange(-rim_width, col_block + rim_width, dtype=jnp.int32)
    rows_inside = (ext_rows >= 0) & (ext_rows < lat_cells)
    cols_inside = (ext_cols >= 0) & (ext_cols < lon_cells)

    def slot_lookup(ghost_ids):
        return jnp.take(order_row, jnp.clip(ghost_ids, 0, ghost_count - 1))

    rim_slots = (
        slot_lookup(ext_cols),
        slot_lookup(lon_cells + ext_cols),
        slot_lookup(2 * lon_cells + ext_rows),
        slot_lookup(2 * lon_cells + lat_cells + ext_rows),
    )

    def extend(block_field):
        return with_halo(block_field, (("lat", 1), ("lon", 2)), rim_width)

    grown_field = extend(start_field)
    source_view = grown_field[
        :, rim_width : rim_width + row_block + 1, rim_width : rim_width + col_block + 1
    ]
    rows_given = corner_rows[0, 0]
    cols_given = corner_cols[0, 0]
    weights = corner_weights[0, 0]
    corners = (
        source_view[:, rows_given, cols_given],
        source_view[:, rows_given + 1, cols_given],
        source_view[:, rows_given, cols_given + 1],
        source_view[:, rows_given + 1, cols_given + 1],
    )
    mixed_values = bilinear(weights, corners)
    partner = swapped(mixed_values, "patch", 0)
    slot_values = lax.all_gather(partner, ("lat", "lon"), axis=1, tiled=True)
    rim_values = tuple((jnp.take(slot_values, rim_slot, axis=1) for rim_slot in rim_slots))
    top_valid = cols_inside & (lat_index == 0)
    bottom_valid = cols_inside & (lat_index == lat_count - 1)
    left_valid = rows_inside & (lon_index == 0)
    right_valid = rows_inside & (lon_index == lon_count - 1)
    lower_row = rim_width + row_block
    right_col = rim_width + col_block

    def with_ghosts(grown):
        grown = grown.at[:, rim_width - 1].set(
            jnp.where(top_valid[None, :, None], rim_values[0], grown[:, rim_width - 1])
        )
        grown = grown.at[:, lower_row].set(
            jnp.where(bottom_valid[None, :, None], rim_values[1], grown[:, lower_row])
        )
        grown = grown.at[:, :, rim_width - 1].set(
            jnp.where(left_valid[None, :, None], rim_values[2], grown[:, :, rim_width - 1])
        )
        grown = grown.at[:, :, right_col].set(
            jnp.where(right_valid[None, :, None], rim_values[3], grown[:, :, right_col])
        )
        return grown

    def relax_colour(grown, colour, margin):
        first_cell = rim_width - margin
        row_end = rim_width + row_block + margin
        col_end = rim_width + col_block + margin
        loop_shift = 1 - margin
        region_rows = row_block + 2 * margin
        region_cols = col_block + 2 * margin
        padded = jnp.pad(grown, ((0, 0), (0, 0), (0, 0), (1, 1)))
        region_coefs = tuple(
            (
                face_coef[
                    loop_shift : loop_shift + region_rows, loop_shift : loop_shift + region_cols
                ]
                for face_coef in loop_coefs
            )
        )
        region_diag = loop_diag[
            loop_shift : loop_shift + region_rows, loop_shift : loop_shift + region_cols
        ]
        relaxed = (force_block + neighbour_sum(padded, region_coefs)) / region_diag
        chosen = (
            loop_parity[
                loop_shift : loop_shift + region_rows, loop_shift : loop_shift + region_cols
            ]
            == colour
        ) & loop_inside[
            loop_shift : loop_shift + region_rows, loop_shift : loop_shift + region_cols
        ]
        updated = jnp.where(chosen[None], relaxed, grown[:, first_cell:row_end, first_cell:col_end])
        return grown.at[:, first_cell:row_end, first_cell:col_end].set(updated)

    def interior(grown):
        return grown[:, rim_width : rim_width + row_block, rim_width : rim_width + col_block]

    current = with_ghosts(grown_field)
    for sweep_index in range(SWEEPS):
        if sweep_index > 0:
            current = with_ghosts(extend(interior(current)))
        current = relax_colour(current, 0, 0)
        current = with_ghosts(extend(interior(current)))
        current = relax_colour(current, 1, 0)
    smoothed = interior(current)
    grown_last = with_ghosts(extend(smoothed))
    padded_last = jnp.pad(grown_last, ((0, 0), (0, 0), (0, 0), (1, 1)))
    inner_coefs = tuple((face_coef[1:-1, 1:-1] for face_coef in loop_coefs))
    inner_diag = loop_diag[1:-1, 1:-1]
    residual_field = force_block - (inner_diag * smoothed - neighbour_sum(padded_last, inner_coefs))
    half_rows = row_block // 2
    half_cols = col_block // 2
    half_levels = levels // 2
    coarse_rhs = residual_field.reshape(3, half_rows, 2, half_cols, 2, half_levels, 2).mean(
        axis=(2, 4, 6)
    )
    coarse_visc = visc_ext.reshape(half_rows + 2, 2, half_cols + 2, 2, half_levels + 2, 2).mean(
        axis=(1, 3, 5)
    )
    coarse_coefs = face_terms(coarse_visc, 0.125)
    coarse_diag = diagonal_of(coarse_coefs)
    coarse_error = RELAX * coarse_rhs / coarse_diag
    for turn_index in range(COARSE - 1):
        coarse_grown = with_halo(coarse_error, (("lat", 1), ("lon", 2)), 1)
        coarse_pad = jnp.pad(coarse_grown, ((0, 0), (0, 0), (0, 0), (1, 1)))
        coarse_error = (
            coarse_error
            + RELAX
            * (coarse_rhs - (coarse_diag * coarse_error - neighbour_sum(coarse_pad, coarse_coefs)))
            / coarse_diag
        )
    correction = jnp.repeat(jnp.repeat(jnp.repeat(coarse_error, 2, axis=1), 2, axis=2), 2, axis=3)
    new_field = smoothed + correction
    return (new_field[None], residual_field[None])


def solution(mesh):
    placed = (
        P("patch", None, "lat", "lon", None),
        P("patch", None, "lat", "lon", None),
        P("patch", "lat", "lon", None),
        P("patch", None),
        P("patch", "lat", "lon"),
        P("patch", "lat", "lon"),
        P("patch", "lat", None, "lon"),
    )
    return jax.shard_map(
        per_device,
        mesh=mesh,
        in_specs=placed,
        out_specs=(P("patch", None, "lat", "lon", None), P("patch", None, "lat", "lon", None)),
        check_vma=False,
    )
```

profile of v0, /device:TPU:0, one launch (start us, length us, event | category | flops | bytes accessed | tf_op | source)
XLA Modules:
  0.0 300.0 jit_solution(8648382601796627605)
XLA Ops:
  1.4 4.9 %collective-permute-start = (f32[2,8,128]{2,1,0:T(8,128)S(1)}, f32[2,8,128]{2,1,0:T(8,128)S(1)}, u32[]{:S(2)}, u32[]{:S(2)}) collective-permute-start(f32[2,8,128]{2,1,0:T(8,128)S(1)} %get-tuple-element.365), channel_id=1, source_target_pairs={{0,8},{1,9},{2,10},{3,11},{4,12},{5,13},{6,14},{7,15},{16,24},{17,... | collective-permute-start | bytes 24584 | tf_op jit(solution)/shard_map/ppermute | solution.py:20
  8.7 4.5 %collective-permute-start.4 = (f32[3,1,8,128]{3,0,2,1:T(4,128)S(1)}, f32[3,1,8,128]{3,0,2,1:T(4,128)S(1)}, u32[]{:S(2)}, u32[]{:S(2)}) collective-permute-start(f32[3,1,8,128]{3,0,2,1:T(4,128)S(1)} %get-tuple-element.330), channel_id=1, source_target_pairs={{0,8},{1,9},{2,10},{3,11},{4,12},{5,13},{6,14},{7,15},{16,24},{17,... | collective-permute-start | bytes 36872 | tf_op jit(solution)/shard_map/ppermute | solution.py:20
  25.6 4.5 %collective-permute-start.6 = (f32[3,18,1,128]{3,0,2,1:T(4,128)S(1)}, f32[3,18,1,128]{3,0,2,1:T(4,128)S(1)}, u32[]{:S(2)}, u32[]{:S(2)}) collective-permute-start(f32[3,18,1,128]{3,0,2,1:T(4,128)S(1)} %get-tuple-element.328), channel_id=1, source_target_pairs={{0,1},{1,2},{2,3},{3,4},{4,5},{5,6},{6,7},{8,9},{9,10},{10,11},{11... | collective-permute-start | bytes 82952 | tf_op jit(solution)/shard_map/ppermute | solution.py:20
  40.6 43.7 %all_gather.3 = f32[3,192,128]{2,0,1:T(4,128)S(1)} all-gather(f32[3,12,128]{2,0,1:T(4,128)S(1)} %collective-permute-done.8), channel_id=1, replica_groups=mesh['patch'=2,'lat'=2,'lon'=8] {'lat','lon'}, dimensions={1}, use_global_device_ids=true | all-gather | bytes 313344 | tf_op jit(solution)/shard_map/all_gather | solution.py:145
  90.6 4.2 %collective-permute-done.10 = f32[3,1,8,128]{3,2,1,0:T(8,128)S(1)} collective-permute-done((f32[3,1,8,128]{3,2,1,0:T(8,128)S(1)}, f32[3,1,8,128]{3,2,1,0:T(8,128)S(1)}, u32[]{:S(2)}, u32[]{:S(2)}) %collective-permute-start.10) | collective-permute-done | bytes 12320 | tf_op jit(solution)/shard_map/ppermute | solution.py:21
  97.7 4.2 %collective-permute-done.12 = f32[3,18,1,128]{3,2,1,0:T(1,128)S(1)} collective-permute-done((f32[3,18,1,128]{3,2,1,0:T(1,128)S(1)}, f32[3,18,1,128]{3,2,1,0:T(1,128)S(1)}, u32[]{:S(2)}, u32[]{:S(2)}) %collective-permute-start.12) | collective-permute-done | bytes 27680 | tf_op jit(solution)/shard_map/ppermute | solution.py:21
  106.1 4.2 %collective-permute-done.14 = f32[3,1,8,128]{3,2,1,0:T(8,128)S(1)} collective-permute-done((f32[3,1,8,128]{3,2,1,0:T(8,128)S(1)}, f32[3,1,8,128]{3,2,1,0:T(8,128)S(1)}, u32[]{:S(2)}, u32[]{:S(2)}) %collective-permute-start.14) | collective-permute-done | bytes 12320 | tf_op jit(solution)/shard_map/ppermute | solution.py:21
  114.6 4.2 %collective-permute-done.16 = f32[3,18,1,128]{3,2,1,0:T(1,128)S(1)} collective-permute-done((f32[3,18,1,128]{3,2,1,0:T(1,128)S(1)}, f32[3,18,1,128]{3,2,1,0:T(1,128)S(1)}, u32[]{:S(2)}, u32[]{:S(2)}) %collective-permute-start.16) | collective-permute-done | bytes 27680 | tf_op jit(solution)/shard_map/ppermute | solution.py:21
  123.0 4.2 %collective-permute-done.18 = f32[3,1,8,128]{3,2,1,0:T(8,128)S(1)} collective-permute-done((f32[3,1,8,128]{3,2,1,0:T(8,128)S(1)}, f32[3,1,8,128]{3,2,1,0:T(8,128)S(1)}, u32[]{:S(2)}, u32[]{:S(2)}) %collective-permute-start.18) | collective-permute-done | bytes 12320 | tf_op jit(solution)/shard_map/ppermute | solution.py:21
  131.5 4.8 %reshape.1229 = f32[10,2,6,2,66,2]{5,4,1,0,3,2:T(8,128)} reshape(f32[20,12,132]{2,0,1:T(8,128)S(1)} %pad_maximum_fusion.8) | data formatting | bytes 253440 | tf_op jit(solution)/shard_map/reshape | solution.py:222
  136.3 4.6 %reduce_sum.19 = f32[10,6,66]{2,0,1:T(8,128)S(1)} reduce(f32[10,2,6,2,66,2]{5,4,1,0,3,2:T(8,128)} %reshape.1229, f32[]{:T(128)} %constant.667.clone.1), dimensions={1,3,5}, to_apply=%region_1.6 | reduce | flops 27720 | bytes 142564 | tf_op jit(solution)/shard_map/reduce_sum | solution.py:222
  145.1 4.2 %collective-permute-done.22 = f32[3,1,8,128]{3,2,1,0:T(8,128)S(1)} collective-permute-done((f32[3,1,8,128]{3,2,1,0:T(8,128)S(1)}, f32[3,1,8,128]{3,2,1,0:T(8,128)S(1)}, u32[]{:S(2)}, u32[]{:S(2)}) %collective-permute-start.22) | collective-permute-done | bytes 12320 | tf_op jit(solution)/shard_map/ppermute | solution.py:21
  149.3 4.5 %collective-permute-start.23 = (f32[3,18,1,128]{3,2,1,0:T(1,128)S(1)}, f32[3,18,1,128]{3,2,1,0:T(1,128)S(1)}, u32[]{:S(2)}, u32[]{:S(2)}) collective-permute-start(f32[3,18,1,128]{3,2,1,0:T(1,128)S(1)} %get-tuple-element.332), channel_id=1, source_target_pairs={{0,1},{1,2},{2,3},{3,4},{4,5},{5,6},{6,7},{8,9},{9,10},{10,11},{11... | collective-permute-start | bytes 82952 | tf_op jit(solution)/shard_map/ppermute | solution.py:20
  155.4 4.2 %collective-permute-done.24 = f32[3,18,1,128]{3,2,1,0:T(1,128)S(1)} collective-permute-done((f32[3,18,1,128]{3,2,1,0:T(1,128)S(1)}, f32[3,18,1,128]{3,2,1,0:T(1,128)S(1)}, u32[]{:S(2)}, u32[]{:S(2)}) %collective-permute-start.24) | collective-permute-done | bytes 27680 | tf_op jit(solution)/shard_map/ppermute | solution.py:21
  160.9 14.0 %reshape.1228 = f32[3,8,2,4,2,64,2]{6,5,4,3,2,1,0:T(8,128)} reshape(f32[3,16,8,128]{3,2,1,0:T(8,128)S(1)} %fusion.27) | data formatting | bytes 393216 | tf_op jit(solution)/shard_map/reshape | solution.py:219
  174.9 5.5 %reduce_sum.18 = f32[3,8,4,64]{3,2,1,0:T(4,128)S(1)} reduce(f32[3,8,2,4,2,64,2]{6,5,4,3,2,1,0:T(8,128)} %reshape.1228, f32[]{:T(128)} %constant.667.clone.1), dimensions={2,4,6}, to_apply=%region_0.5 | reduce | flops 43008 | bytes 221188 | tf_op jit(solution)/shard_map/reduce_sum | solution.py:219
  183.5 4.2 %collective-permute-done.26 = f32[3,1,4,64]{3,2,1,0:T(4,128)S(1)} collective-permute-done((f32[3,1,4,64]{3,2,1,0:T(4,128)S(1)}, f32[3,1,4,64]{3,2,1,0:T(4,128)S(1)}, u32[]{:S(2)}, u32[]{:S(2)}) %collective-permute-start.26) | collective-permute-done | bytes 3104 | tf_op jit(solution)/shard_map/ppermute | solution.py:21
  192.8 4.2 %collective-permute-done.28 = f32[3,10,1,64]{3,2,1,0:T(1,128)S(1)} collective-permute-done((f32[3,10,1,64]{3,2,1,0:T(1,128)S(1)}, f32[3,10,1,64]{3,2,1,0:T(1,128)S(1)}, u32[]{:S(2)}, u32[]{:S(2)}) %collective-permute-start.28) | collective-permute-done | bytes 7712 | tf_op jit(solution)/shard_map/ppermute | solution.py:21
  200.4 4.2 %collective-permute-done.30 = f32[3,1,4,64]{3,2,1,0:T(4,128)S(1)} collective-permute-done((f32[3,1,4,64]{3,2,1,0:T(4,128)S(1)}, f32[3,1,4,64]{3,2,1,0:T(4,128)S(1)}, u32[]{:S(2)}, u32[]{:S(2)}) %collective-permute-start.30) | collective-permute-done | bytes 3104 | tf_op jit(solution)/shard_map/ppermute | solution.py:21
  204.6 4.3 %collective-permute-start.31 = (f32[3,10,1,64]{3,2,1,0:T(1,128)S(1)}, f32[3,10,1,64]{3,2,1,0:T(1,128)S(1)}, u32[]{:S(2)}, u32[]{:S(2)}) collective-permute-start(f32[3,10,1,64]{3,2,1,0:T(1,128)S(1)} %get-tuple-element.377), channel_id=1, source_target_pairs={{0,1},{1,2},{2,3},{3,4},{4,5},{5,6},{6,7},{8,9},{9,10},{10,11},{11... | collective-permute-start | bytes 23048 | tf_op jit(solution)/shard_map/ppermute | solution.py:20
  210.4 4.2 %collective-permute-done.32 = f32[3,10,1,64]{3,2,1,0:T(1,128)S(1)} collective-permute-done((f32[3,10,1,64]{3,2,1,0:T(1,128)S(1)}, f32[3,10,1,64]{3,2,1,0:T(1,128)S(1)}, u32[]{:S(2)}, u32[]{:S(2)}) %collective-permute-start.32) | collective-permute-done | bytes 7712 | tf_op jit(solution)/shard_map/ppermute | solution.py:21
  217.9 4.2 %collective-permute-done.34 = f32[3,1,4,64]{3,2,1,0:T(4,128)S(1)} collective-permute-done((f32[3,1,4,64]{3,2,1,0:T(4,128)S(1)}, f32[3,1,4,64]{3,2,1,0:T(4,128)S(1)}, u32[]{:S(2)}, u32[]{:S(2)}) %collective-permute-start.34) | collective-permute-done | bytes 3104 | tf_op jit(solution)/shard_map/ppermute | solution.py:21
  222.1 4.8 %collective-permute-start.35 = (f32[3,10,1,64]{3,2,1,0:T(1,128)S(1)}, f32[3,10,1,64]{3,2,1,0:T(1,128)S(1)}, u32[]{:S(2)}, u32[]{:S(2)}) collective-permute-start(f32[3,10,1,64]{3,2,1,0:T(1,128)S(1)} %get-tuple-element.375), channel_id=1, source_target_pairs={{0,1},{1,2},{2,3},{3,4},{4,5},{5,6},{6,7},{8,9},{9,10},{10,11},{11... | collective-permute-start | bytes 23048 | tf_op jit(solution)/shard_map/ppermute | solution.py:20
  228.4 4.2 %collective-permute-done.36 = f32[3,10,1,64]{3,2,1,0:T(1,128)S(1)} collective-permute-done((f32[3,10,1,64]{3,2,1,0:T(1,128)S(1)}, f32[3,10,1,64]{3,2,1,0:T(1,128)S(1)}, u32[]{:S(2)}, u32[]{:S(2)}) %collective-permute-start.36) | collective-permute-done | bytes 7712 | tf_op jit(solution)/shard_map/ppermute | solution.py:21
  235.9 4.2 %collective-permute-done.38 = f32[3,1,4,64]{3,2,1,0:T(4,128)S(1)} collective-permute-done((f32[3,1,4,64]{3,2,1,0:T(4,128)S(1)}, f32[3,1,4,64]{3,2,1,0:T(4,128)S(1)}, u32[]{:S(2)}, u32[]{:S(2)}) %collective-permute-start.38) | collective-permute-done | bytes 3104 | tf_op jit(solution)/shard_map/ppermute | solution.py:21
  244.8 4.2 %collective-permute-done.40 = f32[3,10,1,64]{3,2,1,0:T(1,128)S(1)} collective-permute-done((f32[3,10,1,64]{3,2,1,0:T(1,128)S(1)}, f32[3,10,1,64]{3,2,1,0:T(1,128)S(1)}, u32[]{:S(2)}, u32[]{:S(2)}) %collective-permute-start.40) | collective-permute-done | bytes 7712 | tf_op jit(solution)/shard_map/ppermute | solution.py:21
  252.3 4.2 %collective-permute-done.42 = f32[3,1,4,64]{3,2,1,0:T(4,128)S(1)} collective-permute-done((f32[3,1,4,64]{3,2,1,0:T(4,128)S(1)}, f32[3,1,4,64]{3,2,1,0:T(4,128)S(1)}, u32[]{:S(2)}, u32[]{:S(2)}) %collective-permute-start.42) | collective-permute-done | bytes 3104 | tf_op jit(solution)/shard_map/ppermute | solution.py:21
  261.7 4.2 %collective-permute-done.44 = f32[3,10,1,64]{3,2,1,0:T(1,128)S(1)} collective-permute-done((f32[3,10,1,64]{3,2,1,0:T(1,128)S(1)}, f32[3,10,1,64]{3,2,1,0:T(1,128)S(1)}, u32[]{:S(2)}, u32[]{:S(2)}) %collective-permute-start.44) | collective-permute-done | bytes 7712 | tf_op jit(solution)/shard_map/ppermute | solution.py:21
  269.2 4.2 %collective-permute-done.46 = f32[3,1,4,64]{3,2,1,0:T(4,128)S(1)} collective-permute-done((f32[3,1,4,64]{3,2,1,0:T(4,128)S(1)}, f32[3,1,4,64]{3,2,1,0:T(4,128)S(1)}, u32[]{:S(2)}, u32[]{:S(2)}) %collective-permute-start.46) | collective-permute-done | bytes 3104 | tf_op jit(solution)/shard_map/ppermute | solution.py:21
  277.7 4.2 %collective-permute-done.48 = f32[3,10,1,64]{3,2,1,0:T(1,128)S(1)} collective-permute-done((f32[3,10,1,64]{3,2,1,0:T(1,128)S(1)}, f32[3,10,1,64]{3,2,1,0:T(1,128)S(1)}, u32[]{:S(2)}, u32[]{:S(2)}) %collective-permute-start.48) | collective-permute-done | bytes 7712 | tf_op jit(solution)/shard_map/ppermute | solution.py:21
  285.2 4.2 %collective-permute-done.50 = f32[3,1,4,64]{3,2,1,0:T(4,128)S(1)} collective-permute-done((f32[3,1,4,64]{3,2,1,0:T(4,128)S(1)}, f32[3,1,4,64]{3,2,1,0:T(4,128)S(1)}, u32[]{:S(2)}, u32[]{:S(2)}) %collective-permute-start.50) | collective-permute-done | bytes 3104 | tf_op jit(solution)/shard_map/ppermute | solution.py:21
  293.7 4.2 %collective-permute-done.52 = f32[3,10,1,64]{3,2,1,0:T(1,128)S(1)} collective-permute-done((f32[3,10,1,64]{3,2,1,0:T(1,128)S(1)}, f32[3,10,1,64]{3,2,1,0:T(1,128)S(1)}, u32[]{:S(2)}, u32[]{:S(2)}) %collective-permute-start.52) | collective-permute-done | bytes 7712 | tf_op jit(solution)/shard_map/ppermute | solution.py:21
  (286 shorter events, 109.2 us)
Async XLA Ops:
  1.4 18.5 %collective-permute-start = (f32[2,8,128]{2,1,0:T(8,128)S(1)}, f32[2,8,128]{2,1,0:T(8,128)S(1)}, u32[]{:S(2)}, u32[]{:S(2)}) collective-permute-start(f32[2,8,128]{2,1,0:T(8,128)S(1)} %get-tuple-element.365), channel_id=1, source_target_pairs={{0,8},{1,9},{2,10},{3,11},{4,12},{5,13},{6,14},{7,15},{16,24},{17,... | collective-permute-start | bytes 24584 | tf_op jit(solution)/shard_map/ppermute | solution.py:20
  6.3 13.7 %collective-permute-start.1 = (f32[2,8,128]{2,1,0:T(8,128)S(1)}, f32[2,8,128]{2,1,0:T(8,128)S(1)}, u32[]{:S(2)}, u32[]{:S(2)}) collective-permute-start(f32[2,8,128]{2,1,0:T(8,128)S(1)} %get-tuple-element.366), channel_id=1, source_target_pairs={{8,0},{9,1},{10,2},{11,3},{12,4},{13,5},{14,6},{15,7},{24,16},{25,... | collective-permute-start | bytes 24584 | tf_op jit(solution)/shard_map/ppermute | solution.py:21
  8.7 16.9 %collective-permute-start.4 = (f32[3,1,8,128]{3,0,2,1:T(4,128)S(1)}, f32[3,1,8,128]{3,0,2,1:T(4,128)S(1)}, u32[]{:S(2)}, u32[]{:S(2)}) collective-permute-start(f32[3,1,8,128]{3,0,2,1:T(4,128)S(1)} %get-tuple-element.330), channel_id=1, source_target_pairs={{0,8},{1,9},{2,10},{3,11},{4,12},{5,13},{6,14},{7,15},{16,24},{17,... | collective-permute-start | bytes 36872 | tf_op jit(solution)/shard_map/ppermute | solution.py:20
  13.2 12.4 %collective-permute-start.5 = (f32[3,1,8,128]{3,0,2,1:T(4,128)S(1)}, f32[3,1,8,128]{3,0,2,1:T(4,128)S(1)}, u32[]{:S(2)}, u32[]{:S(2)}) collective-permute-start(f32[3,1,8,128]{3,0,2,1:T(4,128)S(1)} %get-tuple-element.331), channel_id=1, source_target_pairs={{8,0},{9,1},{10,2},{11,3},{12,4},{13,5},{14,6},{15,7},{24,16},{25,... | collective-permute-start | bytes 36872 | tf_op jit(solution)/shard_map/ppermute | solution.py:21
  20.9 10.6 %collective-permute-start.2 = (f32[20,2,128]{2,1,0:T(2,128)S(1)}, f32[20,2,128]{2,1,0:T(2,128)S(1)}, u32[]{:S(2)}, u32[]{:S(2)}) collective-permute-start(f32[20,2,128]{2,1,0:T(2,128)S(1)} %get-tuple-element.363), channel_id=1, source_target_pairs={{0,1},{1,2},{2,3},{3,4},{4,5},{5,6},{6,7},{8,9},{9,10},{10,11},{11... | collective-permute-start | bytes 61448 | tf_op jit(solution)/shard_map/ppermute | solution.py:20
  24.3 7.2 %collective-permute-start.3 = (f32[20,2,128]{2,1,0:T(2,128)S(1)}, f32[20,2,128]{2,1,0:T(2,128)S(1)}, u32[]{:S(2)}, u32[]{:S(2)}) collective-permute-start(f32[20,2,128]{2,1,0:T(2,128)S(1)} %get-tuple-element.364), channel_id=1, source_target_pairs={{1,0},{2,1},{3,2},{4,3},{5,4},{6,5},{7,6},{9,8},{10,9},{11,10},{12... | collective-permute-start | bytes 61448 | tf_op jit(solution)/shard_map/ppermute | solution.py:21
  25.6 13.8 %collective-permute-start.6 = (f32[3,18,1,128]{3,0,2,1:T(4,128)S(1)}, f32[3,18,1,128]{3,0,2,1:T(4,128)S(1)}, u32[]{:S(2)}, u32[]{:S(2)}) collective-permute-start(f32[3,18,1,128]{3,0,2,1:T(4,128)S(1)} %get-tuple-element.328), channel_id=1, source_target_pairs={{0,1},{1,2},{2,3},{3,4},{4,5},{5,6},{6,7},{8,9},{9,10},{10,11},{11... | collective-permute-start | bytes 82952 | tf_op jit(solution)/shard_map/ppermute | solution.py:20
  30.2 6.3 %collective-permute-start.7 = (f32[3,18,1,128]{3,0,2,1:T(4,128)S(1)}, f32[3,18,1,128]{3,0,2,1:T(4,128)S(1)}, u32[]{:S(2)}, u32[]{:S(2)}) collective-permute-start(f32[3,18,1,128]{3,0,2,1:T(4,128)S(1)} %get-tuple-element.329), channel_id=1, source_target_pairs={{1,0},{2,1},{3,2},{4,3},{5,4},{6,5},{7,6},{9,8},{10,9},{11,10},{12... | collective-permute-start | bytes 82952 | tf_op jit(solution)/shard_map/ppermute | solution.py:21
  89.3 5.6 %collective-permute-start.10 = (f32[3,1,8,128]{3,2,1,0:T(8,128)S(1)}, f32[3,1,8,128]{3,2,1,0:T(8,128)S(1)}, u32[]{:S(2)}, u32[]{:S(2)}) collective-permute-start(f32[3,1,8,128]{3,2,1,0:T(8,128)S(1)} %get-tuple-element.347), channel_id=1, source_target_pairs={{8,0},{9,1},{10,2},{11,3},{12,4},{13,5},{14,6},{15,7},{24,16},{25,... | collective-permute-start | bytes 36872 | tf_op jit(solution)/shard_map/ppermute | solution.py:21
  96.2 5.8 %collective-permute-start.12 = (f32[3,18,1,128]{3,2,1,0:T(1,128)S(1)}, f32[3,18,1,128]{3,2,1,0:T(1,128)S(1)}, u32[]{:S(2)}, u32[]{:S(2)}) collective-permute-start(f32[3,18,1,128]{3,2,1,0:T(1,128)S(1)} %get-tuple-element.339), channel_id=1, source_target_pairs={{1,0},{2,1},{3,2},{4,3},{5,4},{6,5},{7,6},{9,8},{10,9},{11,10},{12... | collective-permute-start | bytes 82952 | tf_op jit(solution)/shard_map/ppermute | solution.py:21
  104.7 5.6 %collective-permute-start.14 = (f32[3,1,8,128]{3,2,1,0:T(8,128)S(1)}, f32[3,1,8,128]{3,2,1,0:T(8,128)S(1)}, u32[]{:S(2)}, u32[]{:S(2)}) collective-permute-start(f32[3,1,8,128]{3,2,1,0:T(8,128)S(1)} %get-tuple-element.345), channel_id=1, source_target_pairs={{8,0},{9,1},{10,2},{11,3},{12,4},{13,5},{14,6},{15,7},{24,16},{25,... | collective-permute-start | bytes 36872 | tf_op jit(solution)/shard_map/ppermute | solution.py:21
  113.1 5.8 %collective-permute-start.16 = (f32[3,18,1,128]{3,2,1,0:T(1,128)S(1)}, f32[3,18,1,128]{3,2,1,0:T(1,128)S(1)}, u32[]{:S(2)}, u32[]{:S(2)}) collective-permute-start(f32[3,18,1,128]{3,2,1,0:T(1,128)S(1)} %get-tuple-element.337), channel_id=1, source_target_pairs={{1,0},{2,1},{3,2},{4,3},{5,4},{6,5},{7,6},{9,8},{10,9},{11,10},{12... | collective-permute-start | bytes 82952 | tf_op jit(solution)/shard_map/ppermute | solution.py:21
  121.6 5.6 %collective-permute-start.18 = (f32[3,1,8,128]{3,2,1,0:T(8,128)S(1)}, f32[3,1,8,128]{3,2,1,0:T(8,128)S(1)}, u32[]{:S(2)}, u32[]{:S(2)}) collective-permute-start(f32[3,1,8,128]{3,2,1,0:T(8,128)S(1)} %get-tuple-element.343), channel_id=1, source_target_pairs={{8,0},{9,1},{10,2},{11,3},{12,4},{13,5},{14,6},{15,7},{24,16},{25,... | collective-permute-start | bytes 36872 | tf_op jit(solution)/shard_map/ppermute | solution.py:21
  127.2 13.7 %collective-permute-start.19 = (f32[3,18,1,128]{3,2,1,0:T(1,128)S(1)}, f32[3,18,1,128]{3,2,1,0:T(1,128)S(1)}, u32[]{:S(2)}, u32[]{:S(2)}) collective-permute-start(f32[3,18,1,128]{3,2,1,0:T(1,128)S(1)} %get-tuple-element.334), channel_id=1, source_target_pairs={{0,1},{1,2},{2,3},{3,4},{4,5},{5,6},{6,7},{8,9},{9,10},{10,11},{11... | collective-permute-start | bytes 82952 | tf_op jit(solution)/shard_map/ppermute | solution.py:20
  130.0 10.9 %collective-permute-start.20 = (f32[3,18,1,128]{3,2,1,0:T(1,128)S(1)}, f32[3,18,1,128]{3,2,1,0:T(1,128)S(1)}, u32[]{:S(2)}, u32[]{:S(2)}) collective-permute-start(f32[3,18,1,128]{3,2,1,0:T(1,128)S(1)} %get-tuple-element.335), channel_id=1, source_target_pairs={{1,0},{2,1},{3,2},{4,3},{5,4},{6,5},{7,6},{9,8},{10,9},{11,10},{12... | collective-permute-start | bytes 82952 | tf_op jit(solution)/shard_map/ppermute | solution.py:21
  143.7 5.6 %collective-permute-start.22 = (f32[3,1,8,128]{3,2,1,0:T(8,128)S(1)}, f32[3,1,8,128]{3,2,1,0:T(8,128)S(1)}, u32[]{:S(2)}, u32[]{:S(2)}) collective-permute-start(f32[3,1,8,128]{3,2,1,0:T(8,128)S(1)} %get-tuple-element.341), channel_id=1, source_target_pairs={{8,0},{9,1},{10,2},{11,3},{12,4},{13,5},{14,6},{15,7},{24,16},{25,... | collective-permute-start | bytes 36872 | tf_op jit(solution)/shard_map/ppermute | solution.py:21
  149.3 6.1 %collective-permute-start.23 = (f32[3,18,1,128]{3,2,1,0:T(1,128)S(1)}, f32[3,18,1,128]{3,2,1,0:T(1,128)S(1)}, u32[]{:S(2)}, u32[]{:S(2)}) collective-permute-start(f32[3,18,1,128]{3,2,1,0:T(1,128)S(1)} %get-tuple-element.332), channel_id=1, source_target_pairs={{0,1},{1,2},{2,3},{3,4},{4,5},{5,6},{6,7},{8,9},{9,10},{10,11},{11... | collective-permute-start | bytes 82952 | tf_op jit(solution)/shard_map/ppermute | solution.py:20
  153.9 5.8 %collective-permute-start.24 = (f32[3,18,1,128]{3,2,1,0:T(1,128)S(1)}, f32[3,18,1,128]{3,2,1,0:T(1,128)S(1)}, u32[]{:S(2)}, u32[]{:S(2)}) collective-permute-start(f32[3,18,1,128]{3,2,1,0:T(1,128)S(1)} %get-tuple-element.333), channel_id=1, source_target_pairs={{1,0},{2,1},{3,2},{4,3},{5,4},{6,5},{7,6},{9,8},{10,9},{11,10},{12... | collective-permute-start | bytes 82952 | tf_op jit(solution)/shard_map/ppermute | solution.py:21
  182.1 5.5 %collective-permute-start.26 = (f32[3,1,4,64]{3,2,1,0:T(4,128)S(1)}, f32[3,1,4,64]{3,2,1,0:T(4,128)S(1)}, u32[]{:S(2)}, u32[]{:S(2)}) collective-permute-start(f32[3,1,4,64]{3,2,1,0:T(4,128)S(1)} %get-tuple-element.394), channel_id=1, source_target_pairs={{8,0},{9,1},{10,2},{11,3},{12,4},{13,5},{14,6},{15,7},{24,16},{25,... | collective-permute-start | bytes 9224 | tf_op jit(solution)/shard_map/ppermute | solution.py:21
  191.4 5.6 %collective-permute-start.28 = (f32[3,10,1,64]{3,2,1,0:T(1,128)S(1)}, f32[3,10,1,64]{3,2,1,0:T(1,128)S(1)}, u32[]{:S(2)}, u32[]{:S(2)}) collective-permute-start(f32[3,10,1,64]{3,2,1,0:T(1,128)S(1)} %get-tuple-element.380), channel_id=1, source_target_pairs={{1,0},{2,1},{3,2},{4,3},{5,4},{6,5},{7,6},{9,8},{10,9},{11,10},{12... | collective-permute-start | bytes 23048 | tf_op jit(solution)/shard_map/ppermute | solution.py:21
  199.0 5.5 %collective-permute-start.30 = (f32[3,1,4,64]{3,2,1,0:T(4,128)S(1)}, f32[3,1,4,64]{3,2,1,0:T(4,128)S(1)}, u32[]{:S(2)}, u32[]{:S(2)}) collective-permute-start(f32[3,1,4,64]{3,2,1,0:T(4,128)S(1)} %get-tuple-element.392), channel_id=1, source_target_pairs={{8,0},{9,1},{10,2},{11,3},{12,4},{13,5},{14,6},{15,7},{24,16},{25,... | collective-permute-start | bytes 9224 | tf_op jit(solution)/shard_map/ppermute | solution.py:21
  204.6 5.8 %collective-permute-start.31 = (f32[3,10,1,64]{3,2,1,0:T(1,128)S(1)}, f32[3,10,1,64]{3,2,1,0:T(1,128)S(1)}, u32[]{:S(2)}, u32[]{:S(2)}) collective-permute-start(f32[3,10,1,64]{3,2,1,0:T(1,128)S(1)} %get-tuple-element.377), channel_id=1, source_target_pairs={{0,1},{1,2},{2,3},{3,4},{4,5},{5,6},{6,7},{8,9},{9,10},{10,11},{11... | collective-permute-start | bytes 23048 | tf_op jit(solution)/shard_map/ppermute | solution.py:20
  208.9 5.6 %collective-permute-start.32 = (f32[3,10,1,64]{3,2,1,0:T(1,128)S(1)}, f32[3,10,1,64]{3,2,1,0:T(1,128)S(1)}, u32[]{:S(2)}, u32[]{:S(2)}) collective-permute-start(f32[3,10,1,64]{3,2,1,0:T(1,128)S(1)} %get-tuple-element.378), channel_id=1, source_target_pairs={{1,0},{2,1},{3,2},{4,3},{5,4},{6,5},{7,6},{9,8},{10,9},{11,10},{12... | collective-permute-start | bytes 23048 | tf_op jit(solution)/shard_map/ppermute | solution.py:21
  216.6 5.5 %collective-permute-start.34 = (f32[3,1,4,64]{3,2,1,0:T(4,128)S(1)}, f32[3,1,4,64]{3,2,1,0:T(4,128)S(1)}, u32[]{:S(2)}, u32[]{:S(2)}) collective-permute-start(f32[3,1,4,64]{3,2,1,0:T(4,128)S(1)} %get-tuple-element.390), channel_id=1, source_target_pairs={{8,0},{9,1},{10,2},{11,3},{12,4},{13,5},{14,6},{15,7},{24,16},{25,... | collective-permute-start | bytes 9224 | tf_op jit(solution)/shard_map/ppermute | solution.py:21
  222.1 6.2 %collective-permute-start.35 = (f32[3,10,1,64]{3,2,1,0:T(1,128)S(1)}, f32[3,10,1,64]{3,2,1,0:T(1,128)S(1)}, u32[]{:S(2)}, u32[]{:S(2)}) collective-permute-start(f32[3,10,1,64]{3,2,1,0:T(1,128)S(1)} %get-tuple-element.375), channel_id=1, source_target_pairs={{0,1},{1,2},{2,3},{3,4},{4,5},{5,6},{6,7},{8,9},{9,10},{10,11},{11... | collective-permute-start | bytes 23048 | tf_op jit(solution)/shard_map/ppermute | solution.py:20
  226.9 5.6 %collective-permute-start.36 = (f32[3,10,1,64]{3,2,1,0:T(1,128)S(1)}, f32[3,10,1,64]{3,2,1,0:T(1,128)S(1)}, u32[]{:S(2)}, u32[]{:S(2)}) collective-permute-start(f32[3,10,1,64]{3,2,1,0:T(1,128)S(1)} %get-tuple-element.376), channel_id=1, source_target_pairs={{1,0},{2,1},{3,2},{4,3},{5,4},{6,5},{7,6},{9,8},{10,9},{11,10},{12... | collective-permute-start | bytes 23048 | tf_op jit(solution)/shard_map/ppermute | solution.py:21
  234.5 5.5 %collective-permute-start.38 = (f32[3,1,4,64]{3,2,1,0:T(4,128)S(1)}, f32[3,1,4,64]{3,2,1,0:T(4,128)S(1)}, u32[]{:S(2)}, u32[]{:S(2)}) collective-permute-start(f32[3,1,4,64]{3,2,1,0:T(4,128)S(1)} %get-tuple-element.388), channel_id=1, source_target_pairs={{8,0},{9,1},{10,2},{11,3},{12,4},{13,5},{14,6},{15,7},{24,16},{25,... | collective-permute-start | bytes 9224 | tf_op jit(solution)/shard_map/ppermute | solution.py:21
  243.4 5.6 %collective-permute-start.40 = (f32[3,10,1,64]{3,2,1,0:T(1,128)S(1)}, f32[3,10,1,64]{3,2,1,0:T(1,128)S(1)}, u32[]{:S(2)}, u32[]{:S(2)}) collective-permute-start(f32[3,10,1,64]{3,2,1,0:T(1,128)S(1)} %get-tuple-element.374), channel_id=1, source_target_pairs={{1,0},{2,1},{3,2},{4,3},{5,4},{6,5},{7,6},{9,8},{10,9},{11,10},{12... | collective-permute-start | bytes 23048 | tf_op jit(solution)/shard_map/ppermute | solution.py:21
  251.0 5.5 %collective-permute-start.42 = (f32[3,1,4,64]{3,2,1,0:T(4,128)S(1)}, f32[3,1,4,64]{3,2,1,0:T(4,128)S(1)}, u32[]{:S(2)}, u32[]{:S(2)}) collective-permute-start(f32[3,1,4,64]{3,2,1,0:T(4,128)S(1)} %get-tuple-element.386), channel_id=1, source_target_pairs={{8,0},{9,1},{10,2},{11,3},{12,4},{13,5},{14,6},{15,7},{24,16},{25,... | collective-permute-start | bytes 9224 | tf_op jit(solution)/shard_map/ppermute | solution.py:21
  260.2 5.6 %collective-permute-start.44 = (f32[3,10,1,64]{3,2,1,0:T(1,128)S(1)}, f32[3,10,1,64]{3,2,1,0:T(1,128)S(1)}, u32[]{:S(2)}, u32[]{:S(2)}) collective-permute-start(f32[3,10,1,64]{3,2,1,0:T(1,128)S(1)} %get-tuple-element.372), channel_id=1, source_target_pairs={{1,0},{2,1},{3,2},{4,3},{5,4},{6,5},{7,6},{9,8},{10,9},{11,10},{12... | collective-permute-start | bytes 23048 | tf_op jit(solution)/shard_map/ppermute | solution.py:21
  276.2 5.6 %collective-permute-start.48 = (f32[3,10,1,64]{3,2,1,0:T(1,128)S(1)}, f32[3,10,1,64]{3,2,1,0:T(1,128)S(1)}, u32[]{:S(2)}, u32[]{:S(2)}) collective-permute-start(f32[3,10,1,64]{3,2,1,0:T(1,128)S(1)} %get-tuple-element.370), channel_id=1, source_target_pairs={{1,0},{2,1},{3,2},{4,3},{5,4},{6,5},{7,6},{9,8},{10,9},{11,10},{12... | collective-permute-start | bytes 23048 | tf_op jit(solution)/shard_map/ppermute | solution.py:21
  292.2 5.6 %collective-permute-start.52 = (f32[3,10,1,64]{3,2,1,0:T(1,128)S(1)}, f32[3,10,1,64]{3,2,1,0:T(1,128)S(1)}, u32[]{:S(2)}, u32[]{:S(2)}) collective-permute-start(f32[3,10,1,64]{3,2,1,0:T(1,128)S(1)} %get-tuple-element.368), channel_id=1, source_target_pairs={{1,0},{2,1},{3,2},{4,3},{5,4},{6,5},{7,6},{9,8},{10,9},{11,10},{12... | collective-permute-start | bytes 23048 | tf_op jit(solution)/shard_map/ppermute | solution.py:21
  (24 other events, 197.4 us)
where the time goes:
time: 302 us; the launch traced here: 300 us
  starting transfers between devices  106 us (35%)
  waiting for transfers between devices  93 us (31%)
  blocking collectives  43.7 us (14%)
  local copies, waits for them, and re-layouts  34.2 us (11%)
  other arithmetic  21.1 us (7%)
    ppermute x26, waiting for transfers between devices, with_halo(): after = lax.ppermute(first, axis, down)  90.2 us
    ppermute x26, starting transfers between devices, with_halo(): before = lax.ppermute(last, axis, up)  72 us
    all_gather x1, blocking collectives, per_device(): slot_values = lax.all_gather(partner, ('lat', 'lon'), axis=1, tiled=True)  43.7 us
    ppermute x26, starting transfers between devices, with_halo(): after = lax.ppermute(first, axis, down)  33.6 us
    reshape x1, local copies, waits for them, and re-layouts, per_device(): residual_field.reshape(3, half_rows, 2, half_cols, 2, half_levels, 2)  14 us
  transfers between devices with their start and end apart: 53, of which 36 were waited for; matrix products, arithmetic and copies ran while one was open for 8% of the time, Pallas kernels for 0%

commit v1 on v0

v1 whole, which is shorter than its diff:
```python
import functools
import jax
import jax.numpy as jnp
from jax import lax
from jax.experimental import pallas as pl
from jax.experimental.pallas import tpu as pltpu
from jax.sharding import PartitionSpec as P

SWEEPS = 2
COARSE = 8
RELAX = 0.8
MESH = pl.DeviceIdType.MESH


def remote(src, dst, send_sem, recv_sem, device):
    return pltpu.make_async_remote_copy(
        src_ref=src, dst_ref=dst, send_sem=send_sem, recv_sem=recv_sem,
        device_id=device, device_id_type=MESH)


def kernel(sizes, vel, force, visc, slots, rows_in, cols_in, weights, new_out, res_out,
           v, ff, cf, halo, halo_v, srow, rrow, scol, rcol, ssem, rsem,
           sdiag, rdiag, dsem, view, mixed, gathered, gsend, grecv, grow, gcol,
           cvs_row, cvr_row, cvs_col, cvr_col, cvssem, cvrsem,
           ce, cb, cc, chalo, chalo_v, csrow, crrow, cscol, crcol, cssem, crsem):
    rb, cbk, lev, nlat, nlon, q, qrows = sizes
    hr = rb // 2
    n = nlat * nlon
    lat = lax.axis_index("lat")
    lon = lax.axis_index("lon")
    patch = lax.axis_index("patch")
    other = 1 - patch
    me = lat * nlon + lon
    has = (lat > 0, lat < nlat - 1, lon > 0, lon < nlon - 1)
    dev = ({"lat": lat - 1}, {"lat": lat + 1}, {"lon": lon - 1}, {"lon": lon + 1})
    dev_ul = {"lat": lat - 1, "lon": lon - 1}
    dev_dr = {"lat": lat + 1, "lon": lon + 1}
    has_ul = jnp.logical_and(lat > 0, lon > 0)
    has_dr = jnp.logical_and(lat < nlat - 1, lon < nlon - 1)

    barrier = pltpu.get_barrier_semaphore()

    def greet(device):
        pl.semaphore_signal(barrier, inc=1, device_id=device, device_id_type=MESH)

    for side in range(4):
        @pl.when(has[side])
        def _():
            greet(dev[side])

    @pl.when(has_ul)
    def _():
        greet(dev_ul)

    @pl.when(has_dr)
    def _():
        greet(dev_dr)

    def greet_other(k, _):
        t = lax.rem(me + k, n)
        greet({"patch": other, "lat": t // nlon, "lon": lax.rem(t, nlon)})
        return 0

    lax.fori_loop(0, n, greet_other, 0)

    sub = lax.broadcasted_iota(jnp.int32, (1, cbk, lev), 1)
    lane = lax.broadcasted_iota(jnp.int32, (1, cbk, lev), 2)

    def cond(flag, a, b):
        return jnp.where(jnp.full(a.shape, flag.astype(jnp.int32)) == 1, a, b)

    def block(ref, c, rows):
        return ref[pl.ds(c * rows * cbk, rows * cbk), :].reshape(rows, cbk, lev)

    def put(ref, c, rows, value):
        ref[pl.ds(c * rows * cbk, rows * cbk), :] = value.reshape(rows * cbk, lev)

    def pack(k, src, first, count, rows, send_row, send_col):
        for c in range(count):
            o = c * rows * cbk
            f = (first + c)
            send_row[k, 0, pl.ds(f * cbk, cbk), :] = src[pl.ds(o, cbk), :]
            send_row[k, 1, pl.ds(f * cbk, cbk), :] = src[pl.ds(o + (rows - 1) * cbk, cbk), :]
            send_col[k, 0, pl.ds(f * rows, rows), :] = src[pl.ds(o, rows, stride=cbk), :]
            send_col[k, 1, pl.ds(f * rows, rows), :] = src[pl.ds(o + cbk - 1, rows, stride=cbk), :]

    def layer(k, side, count, rows, send_row, recv_row, send_col, recv_col, ss, rs, device):
        back = side ^ 1
        if side < 2:
            m = count * cbk
            return remote(send_row.at[k, back, pl.ds(0, m)], recv_row.at[k, side, pl.ds(0, m)],
                          ss.at[k, back], rs.at[k, side], device)
        m = count * rows
        return remote(send_col.at[k, back - 2, pl.ds(0, m)], recv_col.at[k, side - 2, pl.ds(0, m)],
                      ss.at[k, back], rs.at[k, side], device)

    def start(k, count, rows, *bufs):
        for to in range(4):
            @pl.when(has[to])
            def _():
                layer(k, to ^ 1, count, rows, *bufs, dev[to]).start()

    def arrive(k, count, rows, *bufs):
        for side in range(4):
            @pl.when(has[side])
            def _():
                layer(k, side, count, rows, *bufs, dev[side]).wait_recv()

    def finish(k, count, rows, *bufs):
        for to in range(4):
            @pl.when(has[to])
            def _():
                layer(k, to ^ 1, count, rows, *bufs, dev[to]).wait_send()

    fine = (srow, rrow, scol, rcol, ssem, rsem)
    cvis = (cvs_row, cvr_row, cvs_col, cvr_col, cvssem, cvrsem)
    coarse = (csrow, crrow, cscol, crcol, cssem, crsem)

    pack(0, vel, 0, 3, rb, srow, scol)
    pack(0, visc, 3, 1, rb, srow, scol)
    for c in range(3):
        sdiag[pl.ds(c * cbk, cbk), :] = vel[pl.ds(c * rb * cbk, cbk), :]

    def pair_lane(x):
        return x + jnp.where(lane % 2 == 0, pltpu.roll(x, lev - 1, 2), pltpu.roll(x, 1, 2))

    def pair_sub(x):
        return x + jnp.where(sub % 2 == 0, pltpu.roll(x, cbk - 1, 1), pltpu.roll(x, 1, 1))

    vis = block(visc, 0, rb)
    vis_rows = vis.reshape(hr, 2, cbk, lev)
    vis_rows = vis_rows[:, 0] + vis_rows[:, 1]
    vis_rc = pair_sub(vis_rows)
    vis_rl = pair_lane(vis_rows)
    cvisc = 0.125 * pair_lane(vis_rc)
    put(halo_v, 0, hr, cvisc)
    pack(0, halo_v, 0, 1, hr, cvs_row, cvs_col)

    signals = sum(h.astype(jnp.int32) for h in has) + has_ul.astype(jnp.int32) + has_dr.astype(jnp.int32) + n
    pl.semaphore_wait(barrier, signals)

    start(0, 4, rb, *fine)

    def diagonal_copy(device):
        return remote(sdiag, rdiag, dsem.at[0], dsem.at[1], device)

    @pl.when(has_ul)
    def _():
        diagonal_copy(dev_ul).start()

    start(0, 1, hr, *cvis)

    vr, vc = rb + 1, 2 * cbk
    for c in range(3):
        for r in range(rb):
            view[pl.ds((c * vr + r) * vc, cbk), :] = vel[pl.ds((c * rb + r) * cbk, cbk), :]

    arrive(0, 4, rb, *fine)

    @pl.when(has_dr)
    def _():
        diagonal_copy(dev_dr).wait_recv()

    zero_row = jnp.zeros((cbk, lev), jnp.float32)
    zero_col = jnp.zeros((rb, lev), jnp.float32)
    for c in range(3):
        view[pl.ds((c * vr + rb) * vc, cbk), :] = cond(
            has[1], rrow[0, 1, pl.ds(c * cbk, cbk), :], zero_row)
        view[pl.ds((c * vr + rb) * vc + cbk, cbk), :] = cond(
            has_dr, rdiag[pl.ds(c * cbk, cbk), :], zero_row)
        view[pl.ds(c * vr * vc + cbk, rb, stride=vc), :] = cond(
            has[3], rcol[0, 1, pl.ds(c * rb, rb), :], zero_col)

    for s in range(q):
        base = rows_in[s] * vc + cols_in[s]
        w = [weights[k, s] for k in range(4)]
        for c in range(3):
            o = base + c * vr * vc
            mixed[pl.ds(s * 3 + c, 1), :] = (
                w[0] * view[pl.ds(o, 1), :] + w[1] * view[pl.ds(o + vc, 1), :]
                + w[2] * view[pl.ds(o + 1, 1), :] + w[3] * view[pl.ds(o + vc + 1, 1), :])
    mixed[pl.ds(q * 3, qrows - q * 3), :] = jnp.zeros((qrows - q * 3, lev), jnp.float32)

    def slot_copy(t, source):
        return remote(mixed, gathered.at[pl.ds(pl.multiple_of(source * qrows, 8), qrows)],
                      gsend.at[t], grecv.at[source],
                      {"patch": other, "lat": t // nlon, "lon": lax.rem(t, nlon)})

    def send_slots(k, _):
        slot_copy(lax.rem(me + k, n), me).start()
        return 0

    lax.fori_loop(0, n, send_slots, 0)

    v_up = cond(has[0], rrow[0, 0, pl.ds(3 * cbk, cbk), :], visc[pl.ds(0, cbk), :])
    v_dn = cond(has[1], rrow[0, 1, pl.ds(3 * cbk, cbk), :], visc[pl.ds((rb - 1) * cbk, cbk), :])
    halo[pl.ds(0, rb, stride=cbk), :] = cond(
        has[2], rcol[0, 0, pl.ds(3 * rb, rb), :], scol[0, 0, pl.ds(3 * rb, rb), :])
    halo[pl.ds(cbk - 1, rb, stride=cbk), :] = cond(
        has[3], rcol[0, 1, pl.ds(3 * rb, rb), :], scol[0, 1, pl.ds(3 * rb, rb), :])

    def stack(x, above, below):
        return (jnp.concatenate([above[None], x[:-1]], axis=0),
                jnp.concatenate([x[1:], below[None]], axis=0))

    def beside(x, h):
        return (jnp.where(sub == 0, h, pltpu.roll(x, 1, 1)),
                jnp.where(sub == cbk - 1, h, pltpu.roll(x, cbk - 1, 1)))

    up, dn = stack(vis, v_up, v_dn)
    lf, rt = beside(vis, block(halo, 0, rb))
    bot = jnp.where(lane == 0, vis, pltpu.roll(vis, 1, 2))
    top = jnp.where(lane == lev - 1, vis, pltpu.roll(vis, lev - 1, 2))
    six = [0.5 * (vis + x) for x in (up, dn, lf, rt, bot, top)]
    diag = six[0] + six[1] + six[2] + six[3] + six[4] + six[5]
    inv = 1.0 / diag
    six[4] = jnp.where(lane == 0, 0.0, six[4])
    six[5] = jnp.where(lane == lev - 1, 0.0, six[5])
    for k in range(6):
        put(cf, k, rb, six[k] * inv)
    put(cf, 6, rb, diag)
    for c in range(3):
        put(ff, c, rb, block(force, c, rb) * inv)
        put(v, c, rb, block(vel, c, rb))

    arrive(0, 1, hr, *cvis)
    edge_up = 0.25 * pair_lane(pair_sub(vis[:1]))[0]
    edge_dn = 0.25 * pair_lane(pair_sub(vis[rb - 1:]))[0]
    put(chalo_v, 0, hr, 0.25 * vis_rl)
    edge_lf = chalo_v[pl.ds(0, hr, stride=cbk), :]
    edge_rt = chalo_v[pl.ds(cbk - 1, hr, stride=cbk), :]
    left = cond(has[2], cvr_col[0, 0], edge_lf)
    right = cond(has[3], cvr_col[0, 1], edge_rt)
    for j in range(2):
        chalo[pl.ds(j, hr, stride=cbk), :] = left
        chalo[pl.ds(cbk - 1 - j, hr, stride=cbk), :] = right
    cup, cdn = stack(cvisc, cond(has[0], cvr_row[0, 0], edge_up), cond(has[1], cvr_row[0, 1], edge_dn))

    def beside2(x, h):
        return (jnp.where(sub < 2, h, pltpu.roll(x, 2, 1)),
                jnp.where(sub >= cbk - 2, h, pltpu.roll(x, cbk - 2, 1)))

    clf, crt = beside2(cvisc, block(chalo, 0, hr))
    w = 0.25 * vis_rc
    cbot = jnp.where(lane < 2, jnp.where(lane == 0, w, pltpu.roll(w, 1, 2)), pltpu.roll(cvisc, 2, 2))
    ctop = jnp.where(lane >= lev - 2, jnp.where(lane == lev - 1, w, pltpu.roll(w, lev - 1, 2)),
                     pltpu.roll(cvisc, lev - 2, 2))
    csix = [0.125 * (cvisc + x) for x in (cup, cdn, clf, crt, cbot, ctop)]
    cdiag = csix[0] + csix[1] + csix[2] + csix[3] + csix[4] + csix[5]
    cinv = RELAX / cdiag
    csix[4] = jnp.where(lane < 2, 0.0, csix[4])
    csix[5] = jnp.where(lane >= lev - 2, 0.0, csix[5])
    for k in range(6):
        put(cc, k, hr, csix[k] * cinv)
    put(cc, 6, hr, cinv)

    def slots_arrive(k, _):
        slot_copy(k, k).wait_recv()
        return 0

    lax.fori_loop(0, n, slots_arrive, 0)
    lon_cells = nlon * cbk
    lat_cells = nlat * rb

    def fetch(first, count, out, side):
        for j in range(count):
            s = slots[first + j]
            d = s // q
            base = d * qrows + (s - d * q) * 3
            for c in range(3):
                out[side, pl.ds(c * count + j, 1), :] = gathered[pl.ds(base + c, 1), :]

    for side, first, count, out in (
            (0, lon * cbk, cbk, grow), (1, lon_cells + lon * cbk, cbk, grow),
            (2, 2 * lon_cells + lat * rb, rb, gcol), (3, 2 * lon_cells + lat_cells + lat * rb, rb, gcol)):
        @pl.when(jnp.logical_not(has[side]))
        def _():
            fetch(first, count, out, side % 2)

    parity = lax.rem(lat * rb + lon * cbk, 2) + lax.broadcasted_iota(jnp.int32, (rb, cbk, lev), 0) + sub + lane
    parity = parity % 2

    def halos(k):
        above, below = [], []
        for c in range(3):
            r = pl.ds(c * cbk, cbk)
            above.append(cond(has[0], rrow[k, 0, r, :], grow[0, r, :]))
            below.append(cond(has[1], rrow[k, 1, r, :], grow[1, r, :]))
            m = pl.ds(c * rb, rb)
            o = c * rb * cbk
            halo[pl.ds(o, rb, stride=cbk), :] = cond(has[2], rcol[k, 0, m, :], gcol[0, m, :])
            halo[pl.ds(o + cbk - 1, rb, stride=cbk), :] = cond(has[3], rcol[k, 1, m, :], gcol[1, m, :])
        return above, below

    def jacobi(x, c, above, below, h, coefs, rows, near, step):
        up, dn = stack(x, above, below)
        lf, rt = near(x, h)
        total = block(coefs, 0, rows) * up + block(coefs, 1, rows) * dn
        total = total + block(coefs, 2, rows) * lf + block(coefs, 3, rows) * rt
        total = total + block(coefs, 4, rows) * pltpu.roll(x, step, 2)
        return total + block(coefs, 5, rows) * pltpu.roll(x, lev - step, 2)

    rounds = 2 * SWEEPS
    for k in range(rounds):
        if k > 0:
            arrive(k, 3, rb, *fine)
        above, below = halos(k)
        for c in range(3):
            x = block(v, c, rb)
            relaxed = block(ff, c, rb) + jacobi(x, c, above[c], below[c], block(halo, c, rb), cf, rb, beside, 1)
            put(v, c, rb, jnp.where(parity == k % 2, relaxed, x))
        pack(k + 1, v, 0, 3, rb, srow, scol)
        start(k + 1, 3, rb, *fine)
    arrive(rounds, 3, rb, *fine)
    above, below = halos(rounds)
    for c in range(3):
        x = block(v, c, rb)
        relaxed = block(ff, c, rb) + jacobi(x, c, above[c], below[c], block(halo, c, rb), cf, rb, beside, 1)
        residual = block(cf, 6, rb) * (relaxed - x)
        put(res_out, c, rb, residual)
        pairs = residual.reshape(hr, 2, cbk, lev)
        rhs = 0.125 * pair_lane(pair_sub(pairs[:, 0] + pairs[:, 1]))
        e = rhs * block(cc, 6, hr)
        put(cb, c, hr, e)
        put(ce, c, hr, e)

    zero = jnp.zeros((cbk, lev), jnp.float32)
    zeros = jnp.zeros((hr, lev), jnp.float32)
    for k in range(COARSE - 1):
        pack(k, ce, 0, 3, hr, csrow, cscol)
        start(k, 3, hr, *coarse)
        arrive(k, 3, hr, *coarse)
        for c in range(3):
            r = pl.ds(c * cbk, cbk)
            m = pl.ds(c * hr, hr)
            o = c * hr * cbk
            left = cond(has[2], crcol[k, 0, m, :], zeros)
            right = cond(has[3], crcol[k, 1, m, :], zeros)
            for j in range(2):
                chalo[pl.ds(o + j, hr, stride=cbk), :] = left
                chalo[pl.ds(o + cbk - 1 - j, hr, stride=cbk), :] = right
            x = block(ce, c, hr)
            put(ce, c, hr, block(cb, c, hr) + (1.0 - RELAX) * x + jacobi(
                x, c, cond(has[0], crrow[k, 0, r, :], zero), cond(has[1], crrow[k, 1, r, :], zero),
                block(chalo, c, hr), cc, hr, beside2, 2))

    for c in range(3):
        e = block(ce, c, hr)
        e = jnp.broadcast_to(e[:, None], (hr, 2, cbk, lev)).reshape(rb, cbk, lev)
        put(new_out, c, rb, block(v, c, rb) + e)

    finish(0, 4, rb, *fine)
    for k in range(rounds):
        finish(k + 1, 3, rb, *fine)
    finish(0, 1, hr, *cvis)
    for k in range(COARSE - 1):
        finish(k, 3, hr, *coarse)

    @pl.when(has_ul)
    def _():
        diagonal_copy(dev_ul).wait_send()

    def slots_sent(k, _):
        slot_copy(k, me).wait_send()
        return 0

    lax.fori_loop(0, n, slots_sent, 0)


def per_device(velocity, forcing, viscosity, ghost_slots, corner_rows, corner_cols, corner_weights):
    _, _, rb, cbk, lev = velocity.shape
    nlat, nlon = lax.axis_size("lat"), lax.axis_size("lon")
    n = nlat * nlon
    q = corner_rows.shape[-1]
    qrows = -(-3 * q // 8) * 8 + (8 if (3 * q) % 8 == 0 else 0)
    hr = rb // 2
    flat = rb * cbk
    rounds = 2 * SWEEPS + 1
    f32 = jnp.float32
    vm = lambda *shape: pltpu.VMEM(shape, f32)
    dma = lambda *shape: pltpu.SemaphoreType.DMA(shape)
    vspec = pl.BlockSpec(memory_space=pltpu.VMEM)
    sspec = pl.BlockSpec(memory_space=pltpu.SMEM)
    ck = COARSE - 1
    new, res = pl.pallas_call(
        functools.partial(kernel, (rb, cbk, lev, nlat, nlon, q, qrows)),
        out_shape=[jax.ShapeDtypeStruct((3 * flat, lev), f32)] * 2,
        in_specs=[vspec] * 3 + [sspec] * 4,
        out_specs=[vspec] * 2,
        scratch_shapes=[
            vm(3 * flat, lev), vm(3 * flat, lev), vm(7 * flat, lev), vm(3 * flat, lev), vm(flat, lev),
            vm(rounds, 2, 4 * cbk, lev), vm(rounds, 2, 4 * cbk, lev),
            vm(rounds, 2, 4 * rb, lev), vm(rounds, 2, 4 * rb, lev),
            dma(rounds, 4), dma(rounds, 4),
            vm(3 * cbk, lev), vm(3 * cbk, lev), dma(2),
            vm(3 * (rb + 1) * 2 * cbk, lev), vm(qrows, lev), vm(n * qrows, lev), dma(n), dma(n),
            vm(2, 3 * cbk, lev), vm(2, 3 * rb, lev),
            vm(1, 2, cbk, lev), vm(1, 2, cbk, lev), vm(1, 2, hr, lev), vm(1, 2, hr, lev), dma(1, 4), dma(1, 4),
            vm(3 * hr * cbk, lev), vm(3 * hr * cbk, lev), vm(7 * hr * cbk, lev), vm(3 * hr * cbk, lev), vm(hr * cbk, lev),
            vm(ck, 2, 3 * cbk, lev), vm(ck, 2, 3 * cbk, lev), vm(ck, 2, 3 * hr, lev), vm(ck, 2, 3 * hr, lev),
            dma(ck, 4), dma(ck, 4),
        ],
        compiler_params=pltpu.CompilerParams(
            collective_id=0, has_side_effects=True, vmem_limit_bytes=32 * 2**20),
    )(velocity.reshape(3 * flat, lev), forcing.reshape(3 * flat, lev), viscosity.reshape(flat, lev),
      ghost_slots[0], corner_rows.reshape(q), corner_cols.reshape(q), corner_weights.reshape(4, q))
    return new.reshape(velocity.shape), res.reshape(velocity.shape)


def solution(mesh):
    placed = (
        P("patch", None, "lat", "lon", None),
        P("patch", None, "lat", "lon", None),
        P("patch", "lat", "lon", None),
        P("patch", None),
        P("patch", "lat", "lon"),
        P("patch", "lat", "lon"),
        P("patch", "lat", None, "lon"),
    )
    return jax.shard_map(
        per_device,
        mesh=mesh,
        in_specs=placed,
        out_specs=(P("patch", None, "lat", "lon", None), P("patch", None, "lat", "lon", None)),
        check_vma=False,
    )
```

time: 302 us -> 62.9 us (0.21)
  starting transfers between devices: 106 us -> 0 us
  waiting for transfers between devices: 93 us -> 0 us
  Pallas kernels: 0 us -> 57.2 us
  blocking collectives: 43.7 us -> 0 us
  local copies, waits for them, and re-layouts: 34.2 us -> 4.73 us
  other arithmetic: 21.1 us -> 0 us
    ppermute x53 -> x0, starting transfers between devices: 106 us -> none  [the longest x26 72 us: with_halo(): before = lax.ppermute(last, axis, up)]
    ppermute x53 -> x0, waiting for transfers between devices: 93 us -> none  [the longest x26 90.2 us: with_halo(): after = lax.ppermute(first, axis, down)]
    pallas_call x0 -> x1, Pallas kernels: none -> 57.2 us  [per_device(): pl.pallas_call(functools.partial(kernel, (rb, cbk, lev, nlat, nlon, q, qr...]
    all_gather x1 -> x0, blocking collectives: 43.7 us -> none  [per_device(): slot_values = lax.all_gather(partner, ('lat', 'lon'), axis=1, tiled=True)]
    reshape x6 -> x0, local copies, waits for them, and re-layouts: 19.7 us -> none  [the longest x1 14 us: per_device(): residual_field.reshape(3, half_rows, 2, half_cols, 2, half_levels, 2)]
    reduce_sum x2 -> x0, other arithmetic: 10.1 us -> none  [the longest x1 5.5 us: per_device(): residual_field.reshape(3, half_rows, 2, half_cols, 2, half_levels, 2)]
    gather x14 -> x0, local copies, waits for them, and re-layouts: 8.84 us -> none  [the longest x4 2.75 us: slot_lookup(): return jnp.take(order_row, jnp.clip(ghost_ids, 0, ghost_count - 1))]
    unnamed x7 -> x16, local copies, waits for them, and re-layouts: 1.09 us -> 4.73 us
  transfers between devices with their start and end apart: 53 -> 0, of which waited for: 36 -> 0; matrix products, arithmetic and copies ran while one was open for 8% -> 0% of each run, Pallas kernels for 0% -> 0%
where the time goes in v1:
time: 62.9 us; the launch traced here: 62.6 us
  Pallas kernels  57.2 us (91%)
  local copies, waits for them, and re-layouts  4.73 us (8%)
  between operations  0.68 us (1%)
    pallas_call x1, Pallas kernels, per_device(): pl.pallas_call(functools.partial(kernel, (rb, cbk, lev, nlat, nlon, q, qr...  57.2 us
    unnamed x16, local copies, waits for them, and re-layouts  4.73 us

profile of v1, /device:TPU:0, one launch (start us, length us, event | category | flops | bytes accessed | tf_op | source)
XLA Modules:
  0.0 62.6 jit_solution(3156579221533406349)
XLA Ops:
  0.6 0.0 copy-start.6
  0.6 0.0 copy-start.3
  0.7 0.0 copy-start.4
  0.7 0.0 copy-start.5
  0.7 0.6 copy-done.6
  1.3 0.0 copy-done.3
  1.3 0.0 copy-done.4
  1.3 0.0 copy-done.5
  1.3 0.0 copy-start
  1.3 0.9 %copy-done = f32[1,3,16,8,128]{4,3,2,1,0:T(8,128)S(1)} copy-done((f32[1,3,16,8,128]{4,3,2,1,0:T(8,128)S(1)}, f32[1,3,16,8,128]{4,3,2,1,0:T(8,128)}, u32[]{:S(2)}) %copy-start) | copy-done | bytes 196632
  2.3 0.0 copy-start.1
  2.3 0.9 %copy-done.1 = f32[1,3,16,8,128]{4,3,2,1,0:T(8,128)S(1)} copy-done((f32[1,3,16,8,128]{4,3,2,1,0:T(8,128)S(1)}, f32[1,3,16,8,128]{4,3,2,1,0:T(8,128)}, u32[]{:S(2)}) %copy-start.1) | copy-done | bytes 196632
  3.2 0.0 copy-start.2
  3.2 0.8 %copy-done.2 = f32[1,16,8,128]{3,2,1,0:T(8,128)S(1)} copy-done((f32[1,16,8,128]{3,2,1,0:T(8,128)S(1)}, f32[1,16,8,128]{3,2,1,0:T(8,128)}, u32[]{:S(2)}) %copy-start.2) | copy-done | bytes 65560
  4.0 57.2 %shard_map.86 = (f32[384,128]{1,0:T(8,128)S(1)}, f32[384,128]{1,0:T(8,128)S(1)}) custom-call(f32[384,128]{1,0:T(8,128)S(1)} %bitcast.9, f32[384,128]{1,0:T(8,128)S(1)} %bitcast.10, f32[128,128]{1,0:T(8,128)S(1)} %bitcast.13, s32[192]{0:T(256)S(1)} %bitcast.15, s32[12]{0:T(128)S(1)} %bitcast.16, s32[12]{0:T(128)S(1)} %bitcast.17, f32[4,12]{1,0:T(4,128)S(1)} %bitcast.14), custom_call_target="tpu_custom_call" | custom-call | tf_op jit(solution)/shard_map/pallas_call | solution.py:385
  61.3 0.7 %copy.11 = f32[1,3,16,8,128]{4,3,2,1,0:T(8,128)} copy(f32[1,3,16,8,128]{4,3,2,1,0:T(8,128)S(1)} %bitcast.12) | data formatting | bytes 393216
  62.0 0.7 %copy.12 = f32[1,3,16,8,128]{4,3,2,1,0:T(8,128)} copy(f32[1,3,16,8,128]{4,3,2,1,0:T(8,128)S(1)} %bitcast.11) | data formatting | bytes 393216
Async XLA Ops:
  0.6 0.7 %copy-start.6 = (s32[1,1,12]{2,1,0:T(1,128)S(1)}, s32[1,1,12]{2,1,0:T(1,128)}, u32[]{:S(2)}) copy-start(s32[1,1,12]{2,1,0:T(1,128)} %param.12) | copy-start | bytes 148
  0.6 0.7 %copy-start.3 = (f32[1,1,4,12]{3,2,1,0:T(4,128)S(1)}, f32[1,1,4,12]{3,2,1,0:T(4,128)}, u32[]{:S(2)}) copy-start(f32[1,1,4,12]{3,2,1,0:T(4,128)} %param.13) | copy-start | bytes 580
  0.7 0.7 %copy-start.4 = (s32[1,192]{1,0:T(1,128)S(1)}, s32[1,192]{1,0:T(1,128)}, u32[]{:S(2)}) copy-start(s32[1,192]{1,0:T(1,128)} %param.10) | copy-start | bytes 2308
  0.7 0.7 %copy-start.5 = (s32[1,1,12]{2,1,0:T(1,128)S(1)}, s32[1,1,12]{2,1,0:T(1,128)}, u32[]{:S(2)}) copy-start(s32[1,1,12]{2,1,0:T(1,128)} %param.11) | copy-start | bytes 148
  1.3 0.9 %copy-start = (f32[1,3,16,8,128]{4,3,2,1,0:T(8,128)S(1)}, f32[1,3,16,8,128]{4,3,2,1,0:T(8,128)}, u32[]{:S(2)}) copy-start(f32[1,3,16,8,128]{4,3,2,1,0:T(8,128)} %param.7) | copy-start | bytes 589828
  2.3 0.9 %copy-start.1 = (f32[1,3,16,8,128]{4,3,2,1,0:T(8,128)S(1)}, f32[1,3,16,8,128]{4,3,2,1,0:T(8,128)}, u32[]{:S(2)}) copy-start(f32[1,3,16,8,128]{4,3,2,1,0:T(8,128)} %param.8) | copy-start | bytes 589828
  3.2 0.8 %copy-start.2 = (f32[1,16,8,128]{3,2,1,0:T(8,128)S(1)}, f32[1,16,8,128]{3,2,1,0:T(8,128)}, u32[]{:S(2)}) copy-start(f32[1,16,8,128]{3,2,1,0:T(8,128)} %param.9) | copy-start | bytes 196612

commit v2 on v1

--- a/solution.py
+++ b/solution.py
@@ -12,6 +12,10 @@
 MESH = pl.DeviceIdType.MESH
 
 
+def box_reach(hr, cw):
+    return -(-COARSE // hr), -(-COARSE // cw)
+
+
 def remote(src, dst, send_sem, recv_sem, device):
     return pltpu.make_async_remote_copy(
         src_ref=src, dst_ref=dst, send_sem=send_sem, recv_sem=recv_sem,
@@ -21,10 +25,12 @@
 def kernel(sizes, vel, force, visc, slots, rows_in, cols_in, weights, new_out, res_out,
            v, ff, cf, halo, halo_v, srow, rrow, scol, rcol, ssem, rsem,
            sdiag, rdiag, dsem, view, mixed, gathered, gsend, grecv, grow, gcol,
-           cvs_row, cvr_row, cvs_col, cvr_col, cvssem, cvrsem,
-           ce, cb, cc, chalo, chalo_v, csrow, crrow, cscol, crcol, cssem, crsem):
+           vbox, vbsend, vbrecv, rbox, rbsend, rbrecv, ce, chalo_v, cvreg, cc, rhs_reg, err_reg):
     rb, cbk, lev, nlat, nlon, q, qrows = sizes
     hr = rb // 2
+    cw = cbk // 2
+    near_lat, near_lon = box_reach(hr, cw)
+    wide = 2 * near_lon + 1
     n = nlat * nlon
     lat = lax.axis_index("lat")
     lon = lax.axis_index("lon")
@@ -43,18 +49,44 @@
     def greet(device):
         pl.semaphore_signal(barrier, inc=1, device_id=device, device_id_type=MESH)
 
-    for side in range(4):
-        @pl.when(has[side])
+    offsets = [(dl, dc) for dl in range(-near_lat, near_lat + 1) for dc in range(-near_lon, near_lon + 1)
+               if (dl, dc) != (0, 0)]
+    offsets.sort(key=lambda o: -abs(o[0]) - abs(o[1]))
+
+    def exists(dl, dc):
+        return ((lat + dl >= 0) & (lat + dl < nlat)) & ((lon + dc >= 0) & (lon + dc < nlon))
+
+    def box_index(dl, dc):
+        return (dl + near_lat) * wide + dc + near_lon
+
+    home = box_index(0, 0)
+    around = [exists(dl, dc) for dl, dc in offsets]
+    for (dl, dc), there in zip(offsets, around):
+        @pl.when(there)
         def _():
-            greet(dev[side])
-
-    @pl.when(has_ul)
-    def _():
-        greet(dev_ul)
-
-    @pl.when(has_dr)
-    def _():
-        greet(dev_dr)
+            greet({"lat": lat + dl, "lon": lon + dc})
+
+    def box_copy(buf, send, recv, dl, dc, target):
+        at = box_index(-dl, -dc)
+        return remote(buf.at[home], buf.at[at], send.at[at], recv.at[at], target)
+
+    def box_start(*bufs):
+        for (dl, dc), there in zip(offsets, around):
+            @pl.when(there)
+            def _():
+                box_copy(*bufs, dl, dc, {"lat": lat + dl, "lon": lon + dc}).start()
+
+    def box_arrive(*bufs):
+        for (dl, dc), there in zip(offsets, around):
+            @pl.when(there)
+            def _():
+                box_copy(*bufs, -dl, -dc, {"lat": lat + dl, "lon": lon + dc}).wait_recv()
+
+    def box_finish(*bufs):
+        for (dl, dc), there in zip(offsets, around):
+            @pl.when(there)
+            def _():
+                box_copy(*bufs, dl, dc, {"lat": lat + dl, "lon": lon + dc}).wait_send()
 
     def greet_other(k, _):
         t = lax.rem(me + k, n)
@@ -113,8 +145,8 @@
                 layer(k, to ^ 1, count, rows, *bufs, dev[to]).wait_send()
 
     fine = (srow, rrow, scol, rcol, ssem, rsem)
-    cvis = (cvs_row, cvr_row, cvs_col, cvr_col, cvssem, cvrsem)
-    coarse = (csrow, crrow, cscol, crcol, cssem, crsem)
+    cvis = (vbox, vbsend, vbrecv)
+    coarse = (rbox, rbsend, rbrecv)
 
     pack(0, vel, 0, 3, rb, srow, scol)
     pack(0, visc, 3, 1, rb, srow, scol)
@@ -133,10 +165,24 @@
     vis_rc = pair_sub(vis_rows)
     vis_rl = pair_lane(vis_rows)
     cvisc = 0.125 * pair_lane(vis_rc)
-    put(halo_v, 0, hr, cvisc)
-    pack(0, halo_v, 0, 1, hr, cvs_row, cvs_col)
-
-    signals = sum(h.astype(jnp.int32) for h in has) + has_ul.astype(jnp.int32) + has_dr.astype(jnp.int32) + n
+    ends = 0.25 * vis_rc
+    marked = jnp.where(lane == 1, pltpu.roll(ends, 1, 2),
+                       jnp.where(lane == lev - 2, pltpu.roll(ends, lev - 1, 2), cvisc))
+    put(halo_v, 0, hr, marked)
+    put(chalo_v, 0, hr, 0.25 * vis_rl)
+    for j in range(cw):
+        vbox[home, pl.ds(j * hr, hr), :] = halo_v[pl.ds(2 * j, hr, stride=cbk), :]
+    vbox[home, pl.ds((cw + 1) * hr, hr), :] = cond(
+        has[2], chalo_v[pl.ds(cbk - 1, hr, stride=cbk), :], chalo_v[pl.ds(0, hr, stride=cbk), :])
+    edge = cond(has[0], 0.25 * pair_lane(pair_sub(vis[rb - 1:]))[0], 0.25 * pair_lane(pair_sub(vis[:1]))[0])
+    vbox[home, pl.ds(cw * hr, cbk), :] = edge
+    cvreg[...] = jnp.ones(cvreg.shape, jnp.float32)
+    for (dl, dc), there in zip(offsets, around):
+        @pl.when(jnp.logical_not(there))
+        def _():
+            rbox[box_index(dl, dc)] = jnp.zeros(rbox.shape[1:], jnp.float32)
+
+    signals = sum(there.astype(jnp.int32) for there in around) + n
     pl.semaphore_wait(barrier, signals)
 
     start(0, 4, rb, *fine)
@@ -148,7 +194,6 @@
     def _():
         diagonal_copy(dev_ul).start()
 
-    start(0, 1, hr, *cvis)
 
     vr, vc = rb + 1, 2 * cbk
     for c in range(3):
@@ -191,6 +236,7 @@
         return 0
 
     lax.fori_loop(0, n, send_slots, 0)
+    box_start(*cvis)
 
     v_up = cond(has[0], rrow[0, 0, pl.ds(3 * cbk, cbk), :], visc[pl.ds(0, cbk), :])
     v_dn = cond(has[1], rrow[0, 1, pl.ds(3 * cbk, cbk), :], visc[pl.ds((rb - 1) * cbk, cbk), :])
@@ -223,36 +269,59 @@
         put(ff, c, rb, block(force, c, rb) * inv)
         put(v, c, rb, block(vel, c, rb))
 
-    arrive(0, 1, hr, *cvis)
-    edge_up = 0.25 * pair_lane(pair_sub(vis[:1]))[0]
-    edge_dn = 0.25 * pair_lane(pair_sub(vis[rb - 1:]))[0]
-    put(chalo_v, 0, hr, 0.25 * vis_rl)
-    edge_lf = chalo_v[pl.ds(0, hr, stride=cbk), :]
-    edge_rt = chalo_v[pl.ds(cbk - 1, hr, stride=cbk), :]
-    left = cond(has[2], cvr_col[0, 0], edge_lf)
-    right = cond(has[3], cvr_col[0, 1], edge_rt)
-    for j in range(2):
-        chalo[pl.ds(j, hr, stride=cbk), :] = left
-        chalo[pl.ds(cbk - 1 - j, hr, stride=cbk), :] = right
-    cup, cdn = stack(cvisc, cond(has[0], cvr_row[0, 0], edge_up), cond(has[1], cvr_row[0, 1], edge_dn))
-
-    def beside2(x, h):
-        return (jnp.where(sub < 2, h, pltpu.roll(x, 2, 1)),
-                jnp.where(sub >= cbk - 2, h, pltpu.roll(x, cbk - 2, 1)))
-
-    clf, crt = beside2(cvisc, block(chalo, 0, hr))
-    w = 0.25 * vis_rc
-    cbot = jnp.where(lane < 2, jnp.where(lane == 0, w, pltpu.roll(w, 1, 2)), pltpu.roll(cvisc, 2, 2))
-    ctop = jnp.where(lane >= lev - 2, jnp.where(lane == lev - 1, w, pltpu.roll(w, lev - 1, 2)),
-                     pltpu.roll(cvisc, lev - 2, 2))
-    csix = [0.125 * (cvisc + x) for x in (cup, cdn, clf, crt, cbot, ctop)]
-    cdiag = csix[0] + csix[1] + csix[2] + csix[3] + csix[4] + csix[5]
-    cinv = RELAX / cdiag
-    csix[4] = jnp.where(lane < 2, 0.0, csix[4])
-    csix[5] = jnp.where(lane >= lev - 2, 0.0, csix[5])
-    for k in range(6):
-        put(cc, k, hr, csix[k] * cinv)
-    put(cc, 6, hr, cinv)
+    box_arrive(*cvis)
+    cols, rows_r = cvreg.shape[0], cvreg.shape[1]
+    first_col, first_row = near_lon * cw, near_lat * hr
+
+    for dl, dc in offsets + [(0, 0)]:
+        @pl.when(exists(dl, dc))
+        def _():
+            for j in range(cw):
+                cvreg[(dc + near_lon) * cw + j, pl.ds((dl + near_lat) * hr, hr), :] = (
+                    vbox[box_index(dl, dc), pl.ds(j * hr, hr), :])
+    for dc in range(-near_lon, near_lon + 1):
+        for at_edge, row in ((lat == 0, first_row - 1), (lat == nlat - 1, first_row + hr)):
+            @pl.when(at_edge & exists(0, dc))
+            def _():
+                for j in range(cw):
+                    cvreg[(dc + near_lon) * cw + j, pl.ds(row, 1), :] = (
+                        vbox[box_index(0, dc), pl.ds(cw * hr + 2 * j, 1), :])
+    for dc in range(-near_lon, near_lon + 1):
+        for at_edge, col in ((lon + dc == 0, (dc + near_lon) * cw - 1),
+                             (lon + dc == nlon - 1, (dc + near_lon + 1) * cw)):
+            if 0 <= col < cols:
+                for dl in range(-near_lat, near_lat + 1):
+                    @pl.when(at_edge & exists(dl, dc))
+                    def _():
+                        cvreg[col, pl.ds((dl + near_lat) * hr, hr), :] = (
+                            vbox[box_index(dl, dc), pl.ds((cw + 1) * hr, hr), :])
+    lane_r = lax.broadcasted_iota(jnp.int32, (1, rows_r, lev), 2)
+    row_r = lat * hr - first_row + lax.broadcasted_iota(jnp.int32, (1, rows_r, lev), 1)
+    rows_ok = (row_r >= 0) & (row_r < nlat * hr)
+
+    def whole(x):
+        return jnp.where(lane_r == 1, pltpu.roll(x, 1, 2),
+                         jnp.where(lane_r == lev - 2, pltpu.roll(x, lev - 1, 2), x))
+
+    for col in range(1, cols - 1):
+        m = cvreg[pl.ds(col, 1)]
+        mid = whole(m)
+        cbot = jnp.where(lane_r == 0, pltpu.roll(m, lev - 1, 2), jnp.where(lane_r == 1, m, pltpu.roll(mid, 2, 2)))
+        ctop = jnp.where(lane_r == lev - 1, pltpu.roll(m, 1, 2),
+                         jnp.where(lane_r == lev - 2, m, pltpu.roll(mid, lev - 2, 2)))
+        csix = [0.125 * (mid + x) for x in (
+            pltpu.roll(mid, 1, 1), pltpu.roll(mid, rows_r - 1, 1),
+            whole(cvreg[pl.ds(col - 1, 1)]), whole(cvreg[pl.ds(col + 1, 1)]), cbot, ctop)]
+        cdiag = csix[0] + csix[1] + csix[2] + csix[3] + csix[4] + csix[5]
+        col_g = lon * cw - first_col + col
+        inside = ((col_g >= 0) & (col_g < nlon * cw)).astype(jnp.int32)
+        keep = rows_ok & (jnp.full(rows_ok.shape, inside) == 1)
+        cinv = jnp.where(keep, RELAX / cdiag, 0.0)
+        csix[4] = jnp.where(lane_r < 2, 0.0, csix[4])
+        csix[5] = jnp.where(lane_r >= lev - 2, 0.0, csix[5])
+        for k in range(6):
+            cc[k, pl.ds(col, 1)] = csix[k] * cinv
+        cc[6, pl.ds(col, 1)] = cinv
 
     def slots_arrive(k, _):
         slot_copy(k, k).wait_recv()
@@ -320,29 +389,44 @@
         put(res_out, c, rb, residual)
         pairs = residual.reshape(hr, 2, cbk, lev)
         rhs = 0.125 * pair_lane(pair_sub(pairs[:, 0] + pairs[:, 1]))
-        e = rhs * block(cc, 6, hr)
-        put(cb, c, hr, e)
-        put(ce, c, hr, e)
-
-    zero = jnp.zeros((cbk, lev), jnp.float32)
-    zeros = jnp.zeros((hr, lev), jnp.float32)
+        put(ce, c, hr, rhs)
+        for j in range(cw // 2):
+            first = ce[pl.ds(c * hr * cbk + 2 * j, hr, stride=cbk), :]
+            second = ce[pl.ds(c * hr * cbk + 2 * (j + cw // 2), hr, stride=cbk), :]
+            rbox[home, pl.ds((c * (cw // 2) + j) * hr, hr), :] = jnp.where(lane[0] % 2 == 0, first, second)
+    box_start(*coarse)
+    box_arrive(*coarse)
+    for dl in range(-near_lat, near_lat + 1):
+        for dc in range(-near_lon, near_lon + 1):
+            r = pl.ds((dl + near_lat) * hr, hr)
+            for c in range(3):
+                for j in range(cw // 2):
+                    both = rbox[box_index(dl, dc), pl.ds((c * (cw // 2) + j) * hr, hr), :]
+                    col = (dc + near_lon) * cw + j
+                    rhs_reg[c, col, r, :] = jnp.where(lane[0] % 2 == 0, both, pltpu.roll(both, 1, 1))
+                    rhs_reg[c, col + cw // 2, r, :] = jnp.where(lane[0] % 2 == 0, pltpu.roll(both, lev - 1, 1), both)
+    for c in range(3):
+        for col in range(1, cols - 1):
+            e = rhs_reg[c, col] * cc[6, col]
+            rhs_reg[c, col] = e
+            err_reg[c, col] = e
     for k in range(COARSE - 1):
-        pack(k, ce, 0, 3, hr, csrow, cscol)
-        start(k, 3, hr, *coarse)
-        arrive(k, 3, hr, *coarse)
+        depth = COARSE - 2 - k
+        lo, hi = first_col - depth, first_col + cw + depth
         for c in range(3):
-            r = pl.ds(c * cbk, cbk)
-            m = pl.ds(c * hr, hr)
-            o = c * hr * cbk
-            left = cond(has[2], crcol[k, 0, m, :], zeros)
-            right = cond(has[3], crcol[k, 1, m, :], zeros)
-            for j in range(2):
-                chalo[pl.ds(o + j, hr, stride=cbk), :] = left
-                chalo[pl.ds(o + cbk - 1 - j, hr, stride=cbk), :] = right
-            x = block(ce, c, hr)
-            put(ce, c, hr, block(cb, c, hr) + (1.0 - RELAX) * x + jacobi(
-                x, c, cond(has[0], crrow[k, 0, r, :], zero), cond(has[1], crrow[k, 1, r, :], zero),
-                block(chalo, c, hr), cc, hr, beside2, 2))
+            x = err_reg[c, pl.ds(lo - 1, hi - lo + 2)]
+            mid = x[1:-1]
+            w = pl.ds(lo, hi - lo)
+            total = rhs_reg[c, w] + (1.0 - RELAX) * mid
+            total = total + cc[0, w] * pltpu.roll(mid, 1, 1) + cc[1, w] * pltpu.roll(mid, rows_r - 1, 1)
+            total = total + cc[2, w] * x[:-2] + cc[3, w] * x[2:]
+            total = total + cc[4, w] * pltpu.roll(mid, 2, 2) + cc[5, w] * pltpu.roll(mid, lev - 2, 2)
+            err_reg[c, w] = total
+    for c in range(3):
+        for j in range(cw):
+            tile = err_reg[c, first_col + j, pl.ds(first_row, hr), :]
+            for twin in range(2):
+                ce[pl.ds(c * hr * cbk + 2 * j + twin, hr, stride=cbk), :] = tile
 
     for c in range(3):
         e = block(ce, c, hr)
@@ -352,9 +436,8 @@
     finish(0, 4, rb, *fine)
     for k in range(rounds):
         finish(k + 1, 3, rb, *fine)
-    finish(0, 1, hr, *cvis)
-    for k in range(COARSE - 1):
-        finish(k, 3, hr, *coarse)
+    box_finish(*cvis)
+    box_finish(*coarse)
 
     @pl.when(has_ul)
     def _():
@@ -381,7 +464,10 @@
     dma = lambda *shape: pltpu.SemaphoreType.DMA(shape)
     vspec = pl.BlockSpec(memory_space=pltpu.VMEM)
     sspec = pl.BlockSpec(memory_space=pltpu.SMEM)
-    ck = COARSE - 1
+    cw = cbk // 2
+    near_lat, near_lon = box_reach(hr, cw)
+    nbox = (2 * near_lat + 1) * (2 * near_lon + 1)
+    cols, rows_r = (2 * near_lon + 1) * cw, (2 * near_lat + 1) * hr
     new, res = pl.pallas_call(
         functools.partial(kernel, (rb, cbk, lev, nlat, nlon, q, qrows)),
         out_shape=[jax.ShapeDtypeStruct((3 * flat, lev), f32)] * 2,
@@ -395,10 +481,9 @@
             vm(3 * cbk, lev), vm(3 * cbk, lev), dma(2),
             vm(3 * (rb + 1) * 2 * cbk, lev), vm(qrows, lev), vm(n * qrows, lev), dma(n), dma(n),
             vm(2, 3 * cbk, lev), vm(2, 3 * rb, lev),
-            vm(1, 2, cbk, lev), vm(1, 2, cbk, lev), vm(1, 2, hr, lev), vm(1, 2, hr, lev), dma(1, 4), dma(1, 4),
-            vm(3 * hr * cbk, lev), vm(3 * hr * cbk, lev), vm(7 * hr * cbk, lev), vm(3 * hr * cbk, lev), vm(hr * cbk, lev),
-            vm(ck, 2, 3 * cbk, lev), vm(ck, 2, 3 * cbk, lev), vm(ck, 2, 3 * hr, lev), vm(ck, 2, 3 * hr, lev),
-            dma(ck, 4), dma(ck, 4),
+            vm(nbox, (cw + 2) * hr, lev), dma(nbox), dma(nbox), vm(nbox, 3 * cw // 2 * hr, lev), dma(nbox), dma(nbox),
+            vm(3 * hr * cbk, lev), vm(hr * cbk, lev), vm(cols, rows_r, lev), vm(7, cols, rows_r, lev),
+            vm(3, cols, rows_r, lev), vm(3, cols, rows_r, lev),
         ],
         compiler_params=pltpu.CompilerParams(
             collective_id=0, has_side_effects=True, vmem_limit_bytes=32 * 2**20),

time: 62.9 us -> 50.5 us (0.80)
  Pallas kernels: 57.2 us -> 44.8 us
    pallas_call x1, Pallas kernels: 57.2 us -> 44.8 us  [per_device(): pl.pallas_call(functools.partial(kernel, (rb, cbk, lev, nlat, nlon, q, qr...]
where the time goes in v2:
time: 50.5 us; the launch traced here: 50.3 us
  Pallas kernels  44.8 us (89%)
  local copies, waits for them, and re-layouts  4.73 us (9%)
  between operations  0.68 us (1%)
    pallas_call x1, Pallas kernels, per_device(): pl.pallas_call(functools.partial(kernel, (rb, cbk, lev, nlat, nlon, q, qr...  44.8 us
    unnamed x16, local copies, waits for them, and re-layouts  4.73 us

profile of v2, /device:TPU:0, one launch (start us, length us, event | category | flops | bytes accessed | tf_op | source)
XLA Modules:
  0.0 50.3 jit_solution(310756081794667945)
XLA Ops:
  0.6 0.0 copy-start.6
  0.6 0.0 copy-start.3
  0.7 0.0 copy-start.4
  0.7 0.0 copy-start.5
  0.7 0.6 %copy-done.6 = s32[1,1,12]{2,1,0:T(1,128)S(1)} copy-done((s32[1,1,12]{2,1,0:T(1,128)S(1)}, s32[1,1,12]{2,1,0:T(1,128)}, u32[]{:S(2)}) %copy-start.6) | copy-done | bytes 72
  1.3 0.0 copy-done.3
  1.3 0.0 copy-done.4
  1.3 0.0 copy-done.5
  1.3 0.0 copy-start
  1.3 0.9 %copy-done = f32[1,3,16,8,128]{4,3,2,1,0:T(8,128)S(1)} copy-done((f32[1,3,16,8,128]{4,3,2,1,0:T(8,128)S(1)}, f32[1,3,16,8,128]{4,3,2,1,0:T(8,128)}, u32[]{:S(2)}) %copy-start) | copy-done | bytes 196632
  2.3 0.0 copy-start.1
  2.3 0.9 %copy-done.1 = f32[1,3,16,8,128]{4,3,2,1,0:T(8,128)S(1)} copy-done((f32[1,3,16,8,128]{4,3,2,1,0:T(8,128)S(1)}, f32[1,3,16,8,128]{4,3,2,1,0:T(8,128)}, u32[]{:S(2)}) %copy-start.1) | copy-done | bytes 196632
  3.2 0.0 copy-start.2
  3.2 0.8 %copy-done.2 = f32[1,16,8,128]{3,2,1,0:T(8,128)S(1)} copy-done((f32[1,16,8,128]{3,2,1,0:T(8,128)S(1)}, f32[1,16,8,128]{3,2,1,0:T(8,128)}, u32[]{:S(2)}) %copy-start.2) | copy-done | bytes 65560
  4.0 44.8 %shard_map.86 = (f32[384,128]{1,0:T(8,128)S(1)}, f32[384,128]{1,0:T(8,128)S(1)}) custom-call(f32[384,128]{1,0:T(8,128)S(1)} %bitcast.9, f32[384,128]{1,0:T(8,128)S(1)} %bitcast.10, f32[128,128]{1,0:T(8,128)S(1)} %bitcast.13, s32[192]{0:T(256)S(1)} %bitcast.15, s32[12]{0:T(128)S(1)} %bitcast.16, s32[12]{0:T(128)S(1)} %bitcast.17, f32[4,12]{1,0:T(4,128)S(1)} %bitcast.14), custom_call_target="tpu_custom_call" | custom-call | tf_op jit(solution)/shard_map/pallas_call | solution.py:471
  48.9 0.7 %copy.11 = f32[1,3,16,8,128]{4,3,2,1,0:T(8,128)} copy(f32[1,3,16,8,128]{4,3,2,1,0:T(8,128)S(1)} %bitcast.12) | data formatting | bytes 393216
  49.6 0.7 %copy.12 = f32[1,3,16,8,128]{4,3,2,1,0:T(8,128)} copy(f32[1,3,16,8,128]{4,3,2,1,0:T(8,128)S(1)} %bitcast.11) | data formatting | bytes 393216
Async XLA Ops:
  0.6 0.7 %copy-start.6 = (s32[1,1,12]{2,1,0:T(1,128)S(1)}, s32[1,1,12]{2,1,0:T(1,128)}, u32[]{:S(2)}) copy-start(s32[1,1,12]{2,1,0:T(1,128)} %param.12) | copy-start | bytes 148
  0.6 0.7 %copy-start.3 = (f32[1,1,4,12]{3,2,1,0:T(4,128)S(1)}, f32[1,1,4,12]{3,2,1,0:T(4,128)}, u32[]{:S(2)}) copy-start(f32[1,1,4,12]{3,2,1,0:T(4,128)} %param.13) | copy-start | bytes 580
  0.7 0.7 %copy-start.4 = (s32[1,192]{1,0:T(1,128)S(1)}, s32[1,192]{1,0:T(1,128)}, u32[]{:S(2)}) copy-start(s32[1,192]{1,0:T(1,128)} %param.10) | copy-start | bytes 2308
  0.7 0.7 %copy-start.5 = (s32[1,1,12]{2,1,0:T(1,128)S(1)}, s32[1,1,12]{2,1,0:T(1,128)}, u32[]{:S(2)}) copy-start(s32[1,1,12]{2,1,0:T(1,128)} %param.11) | copy-start | bytes 148
  1.3 0.9 %copy-start = (f32[1,3,16,8,128]{4,3,2,1,0:T(8,128)S(1)}, f32[1,3,16,8,128]{4,3,2,1,0:T(8,128)}, u32[]{:S(2)}) copy-start(f32[1,3,16,8,128]{4,3,2,1,0:T(8,128)} %param.7) | copy-start | bytes 589828
  2.3 0.9 %copy-start.1 = (f32[1,3,16,8,128]{4,3,2,1,0:T(8,128)S(1)}, f32[1,3,16,8,128]{4,3,2,1,0:T(8,128)}, u32[]{:S(2)}) copy-start(f32[1,3,16,8,128]{4,3,2,1,0:T(8,128)} %param.8) | copy-start | bytes 589828
  3.2 0.8 %copy-start.2 = (f32[1,16,8,128]{3,2,1,0:T(8,128)S(1)}, f32[1,16,8,128]{3,2,1,0:T(8,128)}, u32[]{:S(2)}) copy-start(f32[1,16,8,128]{3,2,1,0:T(8,128)} %param.9) | copy-start | bytes 196612

commit v3 on v2

--- a/solution.py
+++ b/solution.py
@@ -236,7 +236,6 @@
         return 0
 
     lax.fori_loop(0, n, send_slots, 0)
-    box_start(*cvis)
 
     v_up = cond(has[0], rrow[0, 0, pl.ds(3 * cbk, cbk), :], visc[pl.ds(0, cbk), :])
     v_dn = cond(has[1], rrow[0, 1, pl.ds(3 * cbk, cbk), :], visc[pl.ds((rb - 1) * cbk, cbk), :])
@@ -269,59 +268,60 @@
         put(ff, c, rb, block(force, c, rb) * inv)
         put(v, c, rb, block(vel, c, rb))
 
-    box_arrive(*cvis)
     cols, rows_r = cvreg.shape[0], cvreg.shape[1]
     first_col, first_row = near_lon * cw, near_lat * hr
 
-    for dl, dc in offsets + [(0, 0)]:
-        @pl.when(exists(dl, dc))
-        def _():
-            for j in range(cw):
-                cvreg[(dc + near_lon) * cw + j, pl.ds((dl + near_lat) * hr, hr), :] = (
-                    vbox[box_index(dl, dc), pl.ds(j * hr, hr), :])
-    for dc in range(-near_lon, near_lon + 1):
-        for at_edge, row in ((lat == 0, first_row - 1), (lat == nlat - 1, first_row + hr)):
-            @pl.when(at_edge & exists(0, dc))
+    def coarse_coefficients():
+        box_arrive(*cvis)
+        for dl, dc in offsets + [(0, 0)]:
+            @pl.when(exists(dl, dc))
             def _():
                 for j in range(cw):
-                    cvreg[(dc + near_lon) * cw + j, pl.ds(row, 1), :] = (
-                        vbox[box_index(0, dc), pl.ds(cw * hr + 2 * j, 1), :])
-    for dc in range(-near_lon, near_lon + 1):
-        for at_edge, col in ((lon + dc == 0, (dc + near_lon) * cw - 1),
-                             (lon + dc == nlon - 1, (dc + near_lon + 1) * cw)):
-            if 0 <= col < cols:
-                for dl in range(-near_lat, near_lat + 1):
-                    @pl.when(at_edge & exists(dl, dc))
-                    def _():
-                        cvreg[col, pl.ds((dl + near_lat) * hr, hr), :] = (
-                            vbox[box_index(dl, dc), pl.ds((cw + 1) * hr, hr), :])
-    lane_r = lax.broadcasted_iota(jnp.int32, (1, rows_r, lev), 2)
-    row_r = lat * hr - first_row + lax.broadcasted_iota(jnp.int32, (1, rows_r, lev), 1)
-    rows_ok = (row_r >= 0) & (row_r < nlat * hr)
-
-    def whole(x):
-        return jnp.where(lane_r == 1, pltpu.roll(x, 1, 2),
-                         jnp.where(lane_r == lev - 2, pltpu.roll(x, lev - 1, 2), x))
-
-    for col in range(1, cols - 1):
-        m = cvreg[pl.ds(col, 1)]
-        mid = whole(m)
-        cbot = jnp.where(lane_r == 0, pltpu.roll(m, lev - 1, 2), jnp.where(lane_r == 1, m, pltpu.roll(mid, 2, 2)))
-        ctop = jnp.where(lane_r == lev - 1, pltpu.roll(m, 1, 2),
-                         jnp.where(lane_r == lev - 2, m, pltpu.roll(mid, lev - 2, 2)))
-        csix = [0.125 * (mid + x) for x in (
-            pltpu.roll(mid, 1, 1), pltpu.roll(mid, rows_r - 1, 1),
-            whole(cvreg[pl.ds(col - 1, 1)]), whole(cvreg[pl.ds(col + 1, 1)]), cbot, ctop)]
-        cdiag = csix[0] + csix[1] + csix[2] + csix[3] + csix[4] + csix[5]
-        col_g = lon * cw - first_col + col
-        inside = ((col_g >= 0) & (col_g < nlon * cw)).astype(jnp.int32)
-        keep = rows_ok & (jnp.full(rows_ok.shape, inside) == 1)
-        cinv = jnp.where(keep, RELAX / cdiag, 0.0)
-        csix[4] = jnp.where(lane_r < 2, 0.0, csix[4])
-        csix[5] = jnp.where(lane_r >= lev - 2, 0.0, csix[5])
-        for k in range(6):
-            cc[k, pl.ds(col, 1)] = csix[k] * cinv
-        cc[6, pl.ds(col, 1)] = cinv
+                    cvreg[(dc + near_lon) * cw + j, pl.ds((dl + near_lat) * hr, hr), :] = (
+                        vbox[box_index(dl, dc), pl.ds(j * hr, hr), :])
+        for dc in range(-near_lon, near_lon + 1):
+            for at_edge, row in ((lat == 0, first_row - 1), (lat == nlat - 1, first_row + hr)):
+                @pl.when(at_edge & exists(0, dc))
+                def _():
+                    for j in range(cw):
+                        cvreg[(dc + near_lon) * cw + j, pl.ds(row, 1), :] = (
+                            vbox[box_index(0, dc), pl.ds(cw * hr + 2 * j, 1), :])
+        for dc in range(-near_lon, near_lon + 1):
+            for at_edge, col in ((lon + dc == 0, (dc + near_lon) * cw - 1),
+                                 (lon + dc == nlon - 1, (dc + near_lon + 1) * cw)):
+                if 0 <= col < cols:
+                    for dl in range(-near_lat, near_lat + 1):
+                        @pl.when(at_edge & exists(dl, dc))
+                        def _():
+                            cvreg[col, pl.ds((dl + near_lat) * hr, hr), :] = (
+                                vbox[box_index(dl, dc), pl.ds((cw + 1) * hr, hr), :])
+        lane_r = lax.broadcasted_iota(jnp.int32, (1, rows_r, lev), 2)
+        row_r = lat * hr - first_row + lax.broadcasted_iota(jnp.int32, (1, rows_r, lev), 1)
+        rows_ok = (row_r >= 0) & (row_r < nlat * hr)
+
+        def whole(x):
+            return jnp.where(lane_r == 1, pltpu.roll(x, 1, 2),
+                             jnp.where(lane_r == lev - 2, pltpu.roll(x, lev - 1, 2), x))
+
+        for col in range(1, cols - 1):
+            m = cvreg[pl.ds(col, 1)]
+            mid = whole(m)
+            cbot = jnp.where(lane_r == 0, pltpu.roll(m, lev - 1, 2), jnp.where(lane_r == 1, m, pltpu.roll(mid, 2, 2)))
+            ctop = jnp.where(lane_r == lev - 1, pltpu.roll(m, 1, 2),
+                             jnp.where(lane_r == lev - 2, m, pltpu.roll(mid, lev - 2, 2)))
+            csix = [0.125 * (mid + x) for x in (
+                pltpu.roll(mid, 1, 1), pltpu.roll(mid, rows_r - 1, 1),
+                whole(cvreg[pl.ds(col - 1, 1)]), whole(cvreg[pl.ds(col + 1, 1)]), cbot, ctop)]
+            cdiag = csix[0] + csix[1] + csix[2] + csix[3] + csix[4] + csix[5]
+            col_g = lon * cw - first_col + col
+            inside = ((col_g >= 0) & (col_g < nlon * cw)).astype(jnp.int32)
+            keep = rows_ok & (jnp.full(rows_ok.shape, inside) == 1)
+            cinv = jnp.where(keep, RELAX / cdiag, 0.0)
+            csix[4] = jnp.where(lane_r < 2, 0.0, csix[4])
+            csix[5] = jnp.where(lane_r >= lev - 2, 0.0, csix[5])
+            for k in range(6):
+                cc[k, pl.ds(col, 1)] = csix[k] * cinv
+            cc[6, pl.ds(col, 1)] = cinv
 
     def slots_arrive(k, _):
         slot_copy(k, k).wait_recv()
@@ -380,6 +380,10 @@
             put(v, c, rb, jnp.where(parity == k % 2, relaxed, x))
         pack(k + 1, v, 0, 3, rb, srow, scol)
         start(k + 1, 3, rb, *fine)
+        if k == 0:
+            box_start(*cvis)
+        if k == 2 * SWEEPS - 2:
+            coarse_coefficients()
     arrive(rounds, 3, rb, *fine)
     above, below = halos(rounds)
     for c in range(3):

time: 50.5 us -> 46.4 us (0.919)
  Pallas kernels: 44.8 us -> 40.7 us
    pallas_call x1, Pallas kernels: 44.8 us -> 40.7 us  [per_device(): pl.pallas_call(functools.partial(kernel, (rb, cbk, lev, nlat, nlon, q, qr...]
where the time goes in v3:
time: 46.4 us; the launch traced here: 46.1 us
  Pallas kernels  40.7 us (88%)
  local copies, waits for them, and re-layouts  4.73 us (10%)
  between operations  0.68 us (1%)
    pallas_call x1, Pallas kernels, per_device(): pl.pallas_call(functools.partial(kernel, (rb, cbk, lev, nlat, nlon, q, qr...  40.7 us
    unnamed x16, local copies, waits for them, and re-layouts  4.73 us

profile of v3, /device:TPU:0, one launch (start us, length us, event | category | flops | bytes accessed | tf_op | source)
XLA Modules:
  0.0 46.1 jit_solution(2032716530459189195)
XLA Ops:
  0.6 0.0 copy-start.6
  0.6 0.0 copy-start.3
  0.7 0.0 copy-start.4
  0.7 0.0 copy-start.5
  0.7 0.6 %copy-done.6 = s32[1,1,12]{2,1,0:T(1,128)S(1)} copy-done((s32[1,1,12]{2,1,0:T(1,128)S(1)}, s32[1,1,12]{2,1,0:T(1,128)}, u32[]{:S(2)}) %copy-start.6) | copy-done | bytes 72
  1.3 0.0 copy-done.3
  1.3 0.0 copy-done.4
  1.3 0.0 copy-done.5
  1.3 0.0 copy-start
  1.3 0.9 %copy-done = f32[1,3,16,8,128]{4,3,2,1,0:T(8,128)S(1)} copy-done((f32[1,3,16,8,128]{4,3,2,1,0:T(8,128)S(1)}, f32[1,3,16,8,128]{4,3,2,1,0:T(8,128)}, u32[]{:S(2)}) %copy-start) | copy-done | bytes 196632
  2.3 0.0 copy-start.1
  2.3 0.9 %copy-done.1 = f32[1,3,16,8,128]{4,3,2,1,0:T(8,128)S(1)} copy-done((f32[1,3,16,8,128]{4,3,2,1,0:T(8,128)S(1)}, f32[1,3,16,8,128]{4,3,2,1,0:T(8,128)}, u32[]{:S(2)}) %copy-start.1) | copy-done | bytes 196632
  3.2 0.0 copy-start.2
  3.2 0.8 %copy-done.2 = f32[1,16,8,128]{3,2,1,0:T(8,128)S(1)} copy-done((f32[1,16,8,128]{3,2,1,0:T(8,128)S(1)}, f32[1,16,8,128]{3,2,1,0:T(8,128)}, u32[]{:S(2)}) %copy-start.2) | copy-done | bytes 65560
  4.0 40.7 %shard_map.86 = (f32[384,128]{1,0:T(8,128)S(1)}, f32[384,128]{1,0:T(8,128)S(1)}) custom-call(f32[384,128]{1,0:T(8,128)S(1)} %bitcast.9, f32[384,128]{1,0:T(8,128)S(1)} %bitcast.10, f32[128,128]{1,0:T(8,128)S(1)} %bitcast.13, s32[192]{0:T(256)S(1)} %bitcast.15, s32[12]{0:T(128)S(1)} %bitcast.16, s32[12]{0:T(128)S(1)} %bitcast.17, f32[4,12]{1,0:T(4,128)S(1)} %bitcast.14), custom_call_target="tpu_custom_call" | custom-call | tf_op jit(solution)/shard_map/pallas_call | solution.py:475
  44.8 0.7 %copy.11 = f32[1,3,16,8,128]{4,3,2,1,0:T(8,128)} copy(f32[1,3,16,8,128]{4,3,2,1,0:T(8,128)S(1)} %bitcast.12) | data formatting | bytes 393216
  45.4 0.7 %copy.12 = f32[1,3,16,8,128]{4,3,2,1,0:T(8,128)} copy(f32[1,3,16,8,128]{4,3,2,1,0:T(8,128)S(1)} %bitcast.11) | data formatting | bytes 393216
Async XLA Ops:
  0.6 0.7 %copy-start.6 = (s32[1,1,12]{2,1,0:T(1,128)S(1)}, s32[1,1,12]{2,1,0:T(1,128)}, u32[]{:S(2)}) copy-start(s32[1,1,12]{2,1,0:T(1,128)} %param.12) | copy-start | bytes 148
  0.6 0.7 %copy-start.3 = (f32[1,1,4,12]{3,2,1,0:T(4,128)S(1)}, f32[1,1,4,12]{3,2,1,0:T(4,128)}, u32[]{:S(2)}) copy-start(f32[1,1,4,12]{3,2,1,0:T(4,128)} %param.13) | copy-start | bytes 580
  0.7 0.7 %copy-start.4 = (s32[1,192]{1,0:T(1,128)S(1)}, s32[1,192]{1,0:T(1,128)}, u32[]{:S(2)}) copy-start(s32[1,192]{1,0:T(1,128)} %param.10) | copy-start | bytes 2308
  0.7 0.7 %copy-start.5 = (s32[1,1,12]{2,1,0:T(1,128)S(1)}, s32[1,1,12]{2,1,0:T(1,128)}, u32[]{:S(2)}) copy-start(s32[1,1,12]{2,1,0:T(1,128)} %param.11) | copy-start | bytes 148
  1.3 0.9 %copy-start = (f32[1,3,16,8,128]{4,3,2,1,0:T(8,128)S(1)}, f32[1,3,16,8,128]{4,3,2,1,0:T(8,128)}, u32[]{:S(2)}) copy-start(f32[1,3,16,8,128]{4,3,2,1,0:T(8,128)} %param.7) | copy-start | bytes 589828
  2.3 0.9 %copy-start.1 = (f32[1,3,16,8,128]{4,3,2,1,0:T(8,128)S(1)}, f32[1,3,16,8,128]{4,3,2,1,0:T(8,128)}, u32[]{:S(2)}) copy-start(f32[1,3,16,8,128]{4,3,2,1,0:T(8,128)} %param.8) | copy-start | bytes 589828
  3.2 0.8 %copy-start.2 = (f32[1,16,8,128]{3,2,1,0:T(8,128)S(1)}, f32[1,16,8,128]{3,2,1,0:T(8,128)}, u32[]{:S(2)}) copy-start(f32[1,16,8,128]{3,2,1,0:T(8,128)} %param.9) | copy-start | bytes 196612
